TPU v7x, 512 devices: a whole 4x8x8 slice. The times are simulated.
512 devices in a mesh: ep: 128 (over y, z, core), tp: 4 (over x).
Axes of the slice: x: 4, y: 8, z: 8, core: 2. Of those that a mesh axis runs over, the one named last changes fastest.
Arguments:
- residual_in: bfloat16 [768, 2048], P('ep'), may hold values from -6 to 6
- new_query: bfloat16 [768, 2048], P('ep', 'tp'), may hold values from -6 to 6
- new_keys: bfloat16 [768, 2048], P('ep', 'tp'), may hold values from -6 to 6
- new_values: bfloat16 [768, 4096], P('ep', 'tp'), may hold values from -6 to 6
- out_gate: bfloat16 [768, 4096], P('ep', 'tp'), may hold values from -6 to 6
- beta_logit: float32 [768, 32], P('ep', 'tp'), may hold values from -6 to 6
- decay_logit: float32 [768, 32], P('ep', 'tp'), may hold values from -6 to 6
- decay_base: float32 [32], P('tp'), may hold values from -1 to 1.5
- decay_bias: float32 [32], P('tp'), may hold values from -2 to 1
- norm_gain: float32 [128], replicated, may hold values from 0.5 to 1.5
- state_store: bfloat16 [768, 32, 128, 128], P('ep', 'tp'), may hold values from -6 to 6
- state_scale: float32 [768, 32], P('ep', 'tp'), may hold values from 0.01 to 0.1
- arrival: int32 [768], P('ep'), may hold values from 0 to 5, as said below
- out_weight: bfloat16 [4096, 2048], P('tp', 'ep'), may hold values from -0.09375 to 0.09375
- ffn_gain: float32 [2048], replicated, may hold values from 0.5 to 1.5
- expert_gate_weight: bfloat16 [256, 2048, 512], P('ep', None, 'tp'), may hold values from -0.125 to 0.125
- expert_up_weight: bfloat16 [256, 2048, 512], P('ep', None, 'tp'), may hold values from -0.125 to 0.125
- expert_down_weight: bfloat16 [256, 512, 2048], P('ep', 'tp'), may hold values from -0.25 to 0.25
- route_ids: int32 [768, 10], P('ep'), may hold values from 0 to 255, as said below
- route_weight: float32 [768, 10], P('ep'), may hold values from 0.02 to 0.3
Outputs:
- mixed: bfloat16 [768, 2048], P('ep', 'tp')
Inputs may be any that keep to these rules, and one draw needn't show every extreme that they name: `arrival`: each aligned block of 6 entries (the requests of one device) is a permutation of 0 to 5. `route_ids`: A row names 10 different experts. Within the rows of one device, an expert is named at most (315) // 256 times, and the experts e with the same e // 2 are named at most 1 times together; that bound is reached.
All inputs are finite; a program needn't handle non-finite values.
Results may differ from a plain program's by a relative error of at most 0.006.
Values may be sent and summed in bfloat16 or wider, within the bound.
A program may use at most 64 MiB of HBM per device.

v0:
```python
import math

import jax
import jax.numpy as jnp
from jax import lax
from jax.sharding import PartitionSpec as P

D = 2048
DK = 128
DV = 128
TOP = 10


def route_tables(route_ids, route_weight, slot_count, peer_slots, owned_experts):
    request_count, top_count = route_ids.shape
    pick_count = request_count * top_count
    flat_ids = route_ids.reshape(pick_count)
    owner_index = flat_ids // owned_experts
    local_expert = flat_ids % owned_experts
    pick_order = jnp.arange(pick_count, dtype=jnp.int32)
    earlier = (owner_index[:, None] == owner_index[None, :]) & (
        pick_order[None, :] < pick_order[:, None]
    )
    slot_index = owner_index * peer_slots + jnp.sum(earlier.astype(jnp.int32), axis=1)
    slot_hit = (jnp.arange(slot_count, dtype=jnp.int32)[:, None] == slot_index[None, :]).astype(
        jnp.float32
    )
    pick_owner = (
        pick_order[:, None] // top_count == jnp.arange(request_count, dtype=jnp.int32)[None, :]
    ).astype(jnp.float32)
    placing = jnp.dot(slot_hit, pick_owner, precision=lax.Precision.HIGHEST)
    slot_flags = jnp.dot(
        slot_hit, local_expert.astype(jnp.float32), precision=lax.Precision.HIGHEST
    )
    weighted_owner = pick_owner * route_weight.reshape(pick_count)[:, None]
    weighting = jnp.dot(weighted_owner.T, slot_hit.T, precision=lax.Precision.HIGHEST)
    return (placing, slot_flags.astype(jnp.bfloat16), weighting)


def expert_masks(flags_in, owned_experts):
    return (
        flags_in.astype(jnp.float32)[None, :]
        == jnp.arange(owned_experts, dtype=jnp.float32)[:, None]
    ).astype(jnp.float32)


def shards(
    residual_in,
    new_query,
    new_keys,
    new_values,
    out_gate,
    beta_logit,
    decay_logit,
    decay_base,
    decay_bias,
    norm_gain,
    state_store,
    state_scale,
    arrival,
    out_weight,
    ffn_gain,
    expert_gate_weight,
    expert_up_weight,
    expert_down_weight,
    route_ids,
    route_weight,
):
    request_count = residual_in.shape[0]
    value_local = new_values.shape[1] // DV
    key_local = new_query.shape[1] // DK
    group_size = value_local // key_local
    query_heads = new_query.astype(jnp.float32).reshape(request_count, key_local, DK)
    query_heads = (
        query_heads
        / jnp.sqrt(jnp.sum(query_heads * query_heads, axis=2, keepdims=True) + 1e-06)
        / math.sqrt(DK)
    )
    key_heads = new_keys.astype(jnp.float32).reshape(request_count, key_local, DK)
    key_heads = key_heads / jnp.sqrt(jnp.sum(key_heads * key_heads, axis=2, keepdims=True) + 1e-06)
    query_heads = jnp.repeat(query_heads, group_size, axis=1)
    key_heads = jnp.repeat(key_heads, group_size, axis=1)
    value_heads = new_values.astype(jnp.float32).reshape(request_count, value_local, DV)
    beta = jax.nn.sigmoid(beta_logit)
    decay = jnp.exp(
        -jnp.exp(decay_base)[None, :] * jax.nn.softplus(decay_logit + decay_bias[None, :])
    )
    stored = jnp.take(state_store, arrival, axis=0)
    stored_scale = jnp.take(state_scale, arrival, axis=0)
    state = stored.astype(jnp.float32) * (stored_scale * decay)[:, :, None, None]
    recalled = jnp.sum(key_heads[:, :, :, None] * state, axis=2)
    delta = beta[:, :, None] * (value_heads - recalled)
    state = state + key_heads[:, :, :, None] * delta[:, :, None, :]
    heads = jnp.sum(query_heads[:, :, :, None] * state, axis=2)
    gate_heads = out_gate.astype(jnp.float32).reshape(request_count, value_local, DV)
    normed_heads = (
        heads
        / jnp.sqrt(jnp.mean(heads * heads, axis=2, keepdims=True) + 1e-06)
        * norm_gain
        * jax.nn.silu(gate_heads)
    )
    gated = normed_heads.reshape(request_count, value_local * DV).astype(jnp.bfloat16)
    projected = jnp.dot(
        lax.all_gather(gated, "ep", axis=0, tiled=True),
        out_weight,
        preferred_element_type=jnp.float32,
    )
    owned_experts = expert_gate_weight.shape[0]
    peer_count = lax.axis_size("ep")
    peer_slots = (request_count * TOP + peer_count - 1) // peer_count
    slot_count = peer_count * peer_slots
    placing, slot_flags, weighting = route_tables(
        route_ids, route_weight, slot_count, peer_slots, owned_experts
    )
    share_width = D // lax.axis_size("tp")
    share_start = lax.axis_index("tp") * share_width
    projected_total = lax.psum(projected, "tp")
    attn_rows = lax.all_to_all(
        projected_total.astype(jnp.bfloat16), "ep", split_axis=0, concat_axis=1, tiled=True
    )
    carried = (residual_in.astype(jnp.float32) + attn_rows.astype(jnp.float32)).astype(jnp.bfloat16)
    carried_wide = carried.astype(jnp.float32)
    normed = (
        carried_wide
        / jnp.sqrt(jnp.mean(carried_wide * carried_wide, axis=1, keepdims=True) + 1e-06)
        * ffn_gain
    ).astype(jnp.bfloat16)
    outgoing = jnp.dot(
        placing.astype(jnp.bfloat16), normed, preferred_element_type=jnp.float32
    ).astype(jnp.bfloat16)
    received_rows, flags_in = (
        lax.all_to_all(outgoing, "ep", split_axis=0, concat_axis=0, tiled=True),
        lax.all_to_all(slot_flags, "ep", split_axis=0, concat_axis=0, tiled=True),
    )
    gate_projected = jnp.einsum(
        "hb,ybk->yhk", received_rows, expert_gate_weight, preferred_element_type=jnp.float32
    )
    up_projected = jnp.einsum(
        "hb,ybk->yhk", received_rows, expert_up_weight, preferred_element_type=jnp.float32
    )
    carried_share = lax.dynamic_slice_in_dim(carried, share_start, share_width, 1)
    masks = expert_masks(flags_in, owned_experts)
    hidden_activation = (jax.nn.silu(gate_projected) * up_projected * masks[:, :, None]).astype(
        jnp.bfloat16
    )
    expert_partial = jnp.einsum(
        "jut,jtx->ux", hidden_activation, expert_down_weight, preferred_element_type=jnp.float32
    )
    expert_share = lax.psum_scatter(expert_partial, "tp", scatter_dimension=1, tiled=True).astype(
        jnp.bfloat16
    )
    returned = lax.all_to_all(expert_share, "ep", split_axis=0, concat_axis=0, tiled=True)
    combined = jnp.dot(weighting, returned.astype(jnp.float32), precision=lax.Precision.HIGHEST)
    return (carried_share.astype(jnp.float32) + combined).astype(jnp.bfloat16)


def solution(mesh):
    return jax.shard_map(
        shards,
        mesh=mesh,
        in_specs=(
            P("ep", None),
            P("ep", "tp"),
            P("ep", "tp"),
            P("ep", "tp"),
            P("ep", "tp"),
            P("ep", "tp"),
            P("ep", "tp"),
            P("tp"),
            P("tp"),
            P(),
            P("ep", "tp", None, None),
            P("ep", "tp"),
            P("ep"),
            P("tp", "ep"),
            P(),
            P("ep", None, "tp"),
            P("ep", None, "tp"),
            P("ep", "tp", None),
            P("ep", None),
            P("ep", None),
        ),
        out_specs=P("ep", "tp"),
        check_vma=False,
    )
```

profile of v0, /device:TPU:1, one launch (start us, length us, event | category | flops | bytes accessed | tf_op | source)
XLA Modules:
  0.0 257.5 jit_solution(16632725009506998111)
XLA Ops:
  6.5 0.8 compare_and_fusion
  7.3 0.7 compare_select_fusion.1
  8.0 0.7 exponential_negate_fusion
  8.6 0.7 reshape.217
  9.6 1.2 gather_fusion.1
  10.9 0.8 gather_fusion
  12.1 1.1 multiply_reduce_fusion.1
  13.4 2.1 multiply_reduce_fusion
  15.7 0.6 fusion.44
  16.9 88.4 %all-gather.3.cloned.1.call-done = bf16[128,6,1024]{2,1,0:T(8,128)(2,1)} async-done(((bf16[1,6,1024]{2,1,0:T(8,128)(2,1)}), bf16[128,6,1024]{2,1,0:T(8,128)(2,1)}) %all-gather.3.cloned.1.call-update) | async-done | bytes 1572880 | tf_op jit(solution)/shard_map/all_gather | solution.py:104
  105.3 2.6 %reshape.241 = bf16[768,1024]{1,0:T(8,128)(2,1)S(1)} reshape(bf16[128,6,1024]{2,1,0:T(8,128)(2,1)} %all-gather.3.cloned.1.call-done) | data formatting | bytes 3145728
  108.4 13.5 %psum.7 = bf16[768,16]{0,1:T(8,128)(2,1)S(1)} all-reduce(f32[768,16]{0,1:T(8,128)S(1)} %fusion.57), channel_id=1, replica_groups=mesh['ep'=128,'tp'=4] {'tp'}, use_global_device_ids=true, to_apply=%region_5.6 | all-reduce | flops 12288 | bytes 73728 | tf_op jit(solution)/shard_map/psum | solution.py:117
  122.1 0.8 all_to_all.32
  122.9 13.4 %all-to-all-start = ((bf16[128,6,16]{2,1,0:T(8,128)(2,1)}), bf16[128,6,16]{2,1,0:T(8,128)(2,1)S(1)}, u32[]{:S(2)}, u32[]{:S(2)}) async-start(bf16[128,6,16]{2,1,0:T(8,128)(2,1)} %all_to_all.32), calls=%async_computation | async-start | bytes 524288 | tf_op jit(solution)/shard_map/all_to_all | solution.py:118
  136.4 0.8 copy.37
  137.3 13.3 %all-to-all-done = bf16[128,6,16]{2,1,0:T(8,128)(2,1)S(1)} async-done(((bf16[128,6,16]{2,1,0:T(8,128)(2,1)}), bf16[128,6,16]{2,1,0:T(8,128)(2,1)S(1)}, u32[]{:S(2)}, u32[]{:S(2)}) %all-to-all-start) | async-done | bytes 24608 | tf_op jit(solution)/shard_map/all_to_all | solution.py:118
  150.5 7.0 %all-to-all-start.2 = ((bf16[128,1,1]{2,1,0:T(2,128)(2,1)}), bf16[128,1,1]{2,1,0:T(2,128)(2,1)S(1)}, u32[]{:S(2)}, u32[]{:S(2)}) async-start(bf16[128,1,1]{2,1,0:T(2,128)(2,1)} %copy.37), calls=%async_computation.2 | async-start | bytes 131072 | tf_op jit(solution)/shard_map/all_to_all | solution.py:133
  158.9 1.0 reduce.2
  159.9 1.2 reshape.249
  161.1 8.1 %all-to-all-done.2 = bf16[128,1,1]{2,1,0:T(2,128)(2,1)S(1)} async-done(((bf16[128,1,1]{2,1,0:T(2,128)(2,1)}), bf16[128,1,1]{2,1,0:T(2,128)(2,1)S(1)}, u32[]{:S(2)}, u32[]{:S(2)}) %all-to-all-start.2) | async-done | bytes 288 | tf_op jit(solution)/shard_map/all_to_all | solution.py:133
  169.2 5.7 %all-to-all-start.1 = ((bf16[128,2,1024]{2,1,0:T(2,128)(2,1)}), bf16[128,2,1024]{2,1,0:T(2,128)(2,1)S(1)}, u32[]{:S(2)}, u32[]{:S(2)}) async-start(bf16[128,2,1024]{2,1,0:T(2,128)(2,1)} %reshape.249), calls=%async_computation.1 | async-start | bytes 1048576 | tf_op jit(solution)/shard_map/all_to_all | solution.py:132
  175.1 1.0 convert_reduce_fusion
  176.2 18.3 %all-to-all-done.1 = bf16[128,2,1024]{2,1,0:T(2,128)(2,1)S(1)} async-done(((bf16[128,2,1024]{2,1,0:T(2,128)(2,1)}), bf16[128,2,1024]{2,1,0:T(2,128)(2,1)S(1)}, u32[]{:S(2)}, u32[]{:S(2)}) %all-to-all-start.1) | async-done | bytes 524320 | tf_op jit(solution)/shard_map/all_to_all | solution.py:132
  194.9 1.7 convolution_bitcast_fusion.2
  196.6 3.3 %convolution_bitcast_fusion = f32[128,2048]{1,0:T(8,128)} fusion(bf16[2,128,2048]{2,1,0:T(8,128)(2,1)} %param.37, bf16[2,2048,128]{2,1,0:T(8,128)(2,1)} %param.36, bf16[128,1,2048]{2,1,0:T(2,128)(2,1)S(1)} %reshape.250, f32[2,128,128]{2,1,0:T(8,128)S(1)} %convolution_bitcast_fusion.2, f32[2,128]{1,0:T(2,128)S(1)} %compare_convert_fusion), kind=kOutput, calls=%fused_computation.5 | convolution fusion | flops 268664832 | bytes 3802112 | tf_op jit(solution)/shard_map/jut,jtx->ux/dot_general | solution.py:146
  200.0 19.7 %reduce-scatter.2.cloned.1.call-done = f32[128,512]{1,0:T(8,128)} async-done(((f32[128,2048]{1,0:T(8,128)}), f32[128,512]{1,0:T(8,128)}) %reduce-scatter.2.cloned.1.call-update) | async-done | bytes 262160 | tf_op jit(solution)/shard_map/reduce_scatter | solution.py:149
  219.6 1.0 convert_bitcast_fusion.1
  220.6 0.7 reduce.3
  221.3 0.7 reshape.251
  221.9 15.7 %all-to-all-start.3 = ((bf16[128,2,256]{2,1,0:T(2,128)(2,1)}), bf16[128,2,256]{2,1,0:T(2,128)(2,1)S(1)}, u32[]{:S(2)}, u32[]{:S(2)}) async-start(bf16[128,2,256]{2,1,0:T(2,128)(2,1)} %reshape.251), calls=%async_computation.4 | async-start | bytes 262144 | tf_op jit(solution)/shard_map/all_to_all | solution.py:152
  238.0 11.9 %all-to-all-done.3 = bf16[128,2,256]{2,1,0:T(2,128)(2,1)S(1)} async-done(((bf16[128,2,256]{2,1,0:T(2,128)(2,1)}), bf16[128,2,256]{2,1,0:T(2,128)(2,1)S(1)}, u32[]{:S(2)}, u32[]{:S(2)}) %all-to-all-start.3) | async-done | bytes 131104 | tf_op jit(solution)/shard_map/all_to_all | solution.py:152
  249.9 0.8 fusion.4
  (69 shorter events, 4.6 us)
Async XLA Ops:
  6.5 4.3 %copy-start = (bf16[6,8,128,128]{3,2,1,0:T(8,128)(2,1)S(1)}, bf16[6,8,128,128]{3,2,1,0:T(8,128)(2,1)}, u32[]{:S(2)}) copy-start(bf16[6,8,128,128]{3,2,1,0:T(8,128)(2,1)} %param.30) | copy-start | bytes 4718596
  6.5 98.7 %all-gather.3.cloned.1.call-start = ((), (), s32[]{:S(2)}) async-start(), calls=%async_computation.6 | async-start | bytes 2113536 | tf_op jit(solution)/shard_map/all_gather | solution.py:104
  10.8 0.9 copy-start.3
  10.8 0.9 copy-start.10
  10.8 0.9 copy-start.5
  10.8 1.2 copy-start.7
  10.9 1.1 copy-start.11
  12.1 3.6 %copy-start.12 = (f32[128]{0:T(128)S(1)}, f32[128]{0:T(128)}, u32[]{:S(2)}) copy-start(f32[128]{0:T(128)} %param.29) | copy-start | bytes 1540
  12.1 3.6 %copy-start.4 = (bf16[6,1024]{1,0:T(8,128)(2,1)S(1)}, bf16[6,1024]{1,0:T(8,128)(2,1)}, u32[]{:S(2)}) copy-start(bf16[6,1024]{1,0:T(8,128)(2,1)} %param.24) | copy-start | bytes 36868
  12.1 4.2 %copy-start.8 = (s32[6,10]{1,0:T(8,128)S(1)}, s32[6,10]{1,0:T(8,128)}, u32[]{:S(2)}) copy-start(s32[6,10]{1,0:T(8,128)} %param.38) | copy-start | bytes 724
  16.9 91.0 %copy-start.1 = (bf16[1024,16]{0,1:T(8,128)(2,1)S(1)}, bf16[1024,16]{0,1:T(8,128)(2,1)}, u32[]{:S(2)}) copy-start(bf16[1024,16]{0,1:T(8,128)(2,1)} %param.33) | copy-start | bytes 98308
  122.1 35.7 %copy-start.2 = (bf16[6,2048]{1,0:T(8,128)(2,1)S(1)}, bf16[6,2048]{1,0:T(8,128)(2,1)}, u32[]{:S(2)}) copy-start(bf16[6,2048]{1,0:T(8,128)(2,1)} %param.20) | copy-start | bytes 73732
  122.9 35.1 %copy-start.6 = (f32[2048]{0:T(1024)S(1)}, f32[2048]{0:T(1024)}, u32[]{:S(2)}) copy-start(f32[2048]{0:T(1024)} %param.34) | copy-start | bytes 24580
  122.9 27.6 %all-to-all-start = ((bf16[128,6,16]{2,1,0:T(8,128)(2,1)}), bf16[128,6,16]{2,1,0:T(8,128)(2,1)S(1)}, u32[]{:S(2)}, u32[]{:S(2)}) async-start(bf16[128,6,16]{2,1,0:T(8,128)(2,1)} %all_to_all.32), calls=%async_computation | async-start | bytes 524288 | tf_op jit(solution)/shard_map/all_to_all | solution.py:118
  150.5 18.6 %all-to-all-start.2 = ((bf16[128,1,1]{2,1,0:T(2,128)(2,1)}), bf16[128,1,1]{2,1,0:T(2,128)(2,1)S(1)}, u32[]{:S(2)}, u32[]{:S(2)}) async-start(bf16[128,1,1]{2,1,0:T(2,128)(2,1)} %copy.37), calls=%async_computation.2 | async-start | bytes 131072 | tf_op jit(solution)/shard_map/all_to_all | solution.py:133
  169.2 25.3 %all-to-all-start.1 = ((bf16[128,2,1024]{2,1,0:T(2,128)(2,1)}), bf16[128,2,1024]{2,1,0:T(2,128)(2,1)S(1)}, u32[]{:S(2)}, u32[]{:S(2)}) async-start(bf16[128,2,1024]{2,1,0:T(2,128)(2,1)} %reshape.249), calls=%async_computation.1 | async-start | bytes 1048576 | tf_op jit(solution)/shard_map/all_to_all | solution.py:132
  174.9 44.7 %reduce-scatter.2.cloned.1.call-start = ((), (), s32[]{:S(2)}) async-start(), calls=%async_computation.5 | async-start | bytes 1310720 | tf_op jit(solution)/shard_map/reduce_scatter | solution.py:149
  199.9 37.7 %copy-start.9 = (f32[6,10]{1,0:T(8,128)S(1)}, f32[6,10]{1,0:T(8,128)}, u32[]{:S(2)}) copy-start(f32[6,10]{1,0:T(8,128)} %param.39) | copy-start | bytes 724
  221.9 27.9 %all-to-all-start.3 = ((bf16[128,2,256]{2,1,0:T(2,128)(2,1)}), bf16[128,2,256]{2,1,0:T(2,128)(2,1)S(1)}, u32[]{:S(2)}, u32[]{:S(2)}) async-start(bf16[128,2,256]{2,1,0:T(2,128)(2,1)} %reshape.251), calls=%async_computation.4 | async-start | bytes 262144 | tf_op jit(solution)/shard_map/all_to_all | solution.py:152
Sparse Core Ops, SparseCore 0:
  16.5 88.7 all-gather.2
  200.1 19.4 reduce-scatter.1
where the time goes:
time: 258 us
  waiting for transfers between devices  160 us (62%)
  starting transfers between devices  42 us (16%)
  between operations  13.8 us (5%)
  blocking collectives  13.5 us (5%)
  other arithmetic  10.7 us (4%)
  local copies, waits for them, and re-layouts  10.6 us (4%)
  matrix products  7.28 us (3%)
    all_gather x1, waiting for transfers between devices, shards(): lax.all_gather(gated, 'ep', axis=0, tiled=True)  88.4 us
    reduce_scatter x1, waiting for transfers between devices, shards(): lax.psum_scatter(expert_partial, 'tp', scatter_dimension=1, tiled=True)  19.7 us
    all_to_all x1, waiting for transfers between devices, shards(): lax.all_to_all(outgoing, 'ep', split_axis=0, concat_axis=0, tiled=True)  18.3 us
    all_to_all x1, starting transfers between devices, shards(): lax.all_to_all(expert_share, 'ep', split_axis=0, concat_axis=0, tiled=True)  15.7 us
    psum x1, blocking collectives, shards(): projected_total = lax.psum(projected, 'tp')  13.5 us
    all_to_all x1, starting transfers between devices, shards(): lax.all_to_all(projected_total.astype(jnp.bfloat16), 'ep', split_axis=0,...  13.4 us
    all_to_all x1, waiting for transfers between devices, shards(): lax.all_to_all(projected_total.astype(jnp.bfloat16), 'ep', split_axis=0,...  13.3 us
    all_to_all x1, waiting for transfers between devices, shards(): lax.all_to_all(expert_share, 'ep', split_axis=0, concat_axis=0, tiled=True)  11.9 us
  transfers between devices with their start and end apart: 6, of which 6 were waited for; matrix products, arithmetic and copies ran while one was open for 2% of the time, Pallas kernels for 0%

commit v1 on v0

v1 whole, which is shorter than its diff:
```python
import functools
import math

import jax
import jax.numpy as jnp
from jax import lax
from jax.experimental import pallas as pl
from jax.experimental.pallas import tpu as pltpu
from jax.sharding import PartitionSpec as P

MESH = pl.DeviceIdType.MESH
F32 = jnp.float32
BF16 = jnp.bfloat16
LANES = 128
PAD = 8
SRC = 2
ROWS = SRC * PAD
NT = (((1,), (1,)), ((), ()))
EXACT = lax.Precision.HIGHEST


def mm(a, b, dims=(((1,), (0,)), ((), ())), precision=None):
    return lax.dot_general(a, b, dims, preferred_element_type=F32, precision=precision)


def iota(shape, axis):
    return lax.broadcasted_iota(jnp.int32, shape, axis)


def silu(v):
    return v * jax.nn.sigmoid(v)


def whole_wait(ref, sem):
    pltpu.make_async_copy(ref, ref, sem).wait()


def kernel(
    nx,
    ny,
    nzc,
    top,
    residual,
    query,
    keys,
    values,
    out_gate,
    beta_logit,
    decay_logit,
    decay_base,
    decay_bias,
    norm_gain,
    state_scale,
    arrival,
    out_weight,
    ffn_gain,
    route_ids,
    route_weight,
    state_hbm,
    gate_hbm,
    up_hbm,
    down_hbm,
    out,
    stage,
    small,
    state,
    w_in,
    w_down,
    w_out,
    r0_src,
    r0_in,
    r1_src,
    r1_in,
    g_src,
    g_in,
    p_src,
    p_in,
    c_src,
    c_in,
    n_scr,
    place,
    weigh,
    masks,
    m3_src,
    m3_in,
    x_src,
    x_in,
    y_own,
    y_src,
    y_in,
    m6_src,
    m6_in,
    m7_src,
    m7_in,
    load_sem,
    send_sem,
    recv_sem,
):
    count, width = residual.shape
    chunks = width // LANES
    y_chunks = chunks // ny
    x_chunks = chunks // nx
    key_heads = query.shape[1] // LANES
    heads = 2 * key_heads
    slots = nzc * SRC
    groups = nzc // 8
    flat = 16 * chunks

    ep = lax.axis_index("ep")
    my_x = lax.axis_index("tp")
    my_y = ep // nzc
    my_zc = lax.rem(ep, nzc)

    def at_y(y):
        return (y * nzc + my_zc, my_x)

    def at_zc(zc):
        return (my_y * nzc + zc, my_x)

    def at_x(x):
        return (ep, x)

    ys = [lax.rem(my_y + d, ny) for d in range(1, ny)]
    zcs = [lax.rem(my_zc + d, nzc) for d in range(1, nzc)]
    xs = [lax.rem(my_x + d, nx) for d in range(1, nx)]

    sent = []

    def send(src, dst, hop, target):
        copy = pltpu.make_async_remote_copy(
            src_ref=src,
            dst_ref=dst,
            send_sem=send_sem.at[hop],
            recv_sem=recv_sem.at[hop],
            device_id=target,
            device_id_type=MESH,
        )
        copy.start()
        sent.append(copy)

    loads = [pltpu.make_async_copy(state_hbm, state, load_sem.at[0])]
    for e in range(2):
        span = pl.ds(e * LANES, LANES)
        loads.append(
            pltpu.make_async_copy(gate_hbm.at[e], w_in.at[:, pl.ds(e * LANES, LANES)], load_sem.at[1 + e])
        )
        loads.append(
            pltpu.make_async_copy(
                up_hbm.at[e], w_in.at[:, pl.ds((2 + e) * LANES, LANES)], load_sem.at[3 + e]
            )
        )
        loads.append(pltpu.make_async_copy(down_hbm.at[e], w_down.at[span, :], load_sem.at[5 + e]))
    for load in loads:
        load.start()

    barrier = pltpu.get_barrier_semaphore()
    greeted = 0
    for zc in zcs:
        pl.semaphore_signal(barrier, inc=1, device_id=at_zc(zc), device_id_type=MESH)
        greeted += 1
    for dx in range(nx):
        for dy in range(ny):
            if dx or dy:
                peer = (lax.rem(my_y + dy, ny) * nzc + my_zc, lax.rem(my_x + dx, nx))
                pl.semaphore_signal(barrier, inc=1, device_id=peer, device_id_type=MESH)
                greeted += 1

    stage[...] = jnp.zeros_like(stage)
    small[...] = jnp.zeros_like(small)
    q_at, k_at, v_at, g_at = 0, key_heads, 2 * key_heads, 2 * key_heads + heads
    r_at = g_at + heads
    for at, ref in ((q_at, query), (k_at, keys), (v_at, values), (g_at, out_gate), (r_at, residual)):
        stage[0:count, at * LANES : at * LANES + ref.shape[1]] = ref[...].astype(F32)

    small[0, 0:count, 0:top] = (route_ids[...] + 1).astype(F32)
    small[1, 0:count, 0:top] = route_weight[...]
    shift = my_y * top
    rolled_ids = pltpu.roll(small[0], shift, 1)
    rolled_weights = pltpu.roll(small[1], shift, 1)
    for y in range(ny):
        r0_src[y, 0:PAD, :] = rolled_ids
        r0_src[y, PAD : 2 * PAD, :] = rolled_weights
        for i in range(y_chunks):
            at = r_at + y * y_chunks + i
            r0_src[y, (2 + i) * PAD : (3 + i) * PAD, :] = stage[:, at * LANES : (at + 1) * LANES]

    own_cols = pl.ds(pl.multiple_of(my_zc * 16, 16), 16)
    eye = (iota((16, 16), 0) == iota((16, 16), 1)).astype(BF16)
    w_out[own_cols, :] = mm(eye, out_weight[...], NT).astype(BF16)
    r0_in[my_y] = r0_src[my_y]

    pl.semaphore_wait(barrier, greeted)

    for y in ys:
        send(r0_src.at[y], r0_in.at[my_y], 0, at_y(y))
    for zc in zcs:
        send(w_out.at[own_cols, :], w_out.at[own_cols, :], 1, at_zc(zc))

    loads[0].wait()
    small[2, 0:count, 0:heads] = decay_logit[...]
    small[3, 0:count, 0:heads] = beta_logit[...]
    rate = jnp.exp(decay_base[...])
    logit = small[2, :, 0:heads] + decay_bias[...]
    soft = jnp.maximum(logit, 0.0) + jnp.log1p(jnp.exp(-jnp.abs(logit)))
    decay = jnp.exp(-rate * soft)
    beta = jax.nn.sigmoid(small[3, :, 0:heads])
    row8 = iota((PAD, 1), 0)
    moved = jnp.zeros((PAD, heads), F32)
    for r in range(count):
        moved = jnp.where(row8 == r, state_scale[pl.ds(arrival[r], 1), :], moved)
    carry = moved * decay
    gain = norm_gain[...]

    for g in range(key_heads):
        q = stage[:, (q_at + g) * LANES : (q_at + g + 1) * LANES]
        k = stage[:, (k_at + g) * LANES : (k_at + g + 1) * LANES]
        q = q * (lax.rsqrt(jnp.sum(q * q, axis=1, keepdims=True) + 1e-06) / math.sqrt(LANES))
        k = k * lax.rsqrt(jnp.sum(k * k, axis=1, keepdims=True) + 1e-06)
        qk = jnp.sum(q * k, axis=1, keepdims=True)
        k_hi = k.astype(BF16).astype(F32)
        q_hi = q.astype(BF16).astype(F32)
        lhs = jnp.concatenate([k_hi, k - k_hi, q_hi, q - q_hi], axis=0).astype(BF16)
        from_k = jnp.zeros((PAD, 2 * LANES), F32)
        from_q = jnp.zeros((PAD, 2 * LANES), F32)
        for r in range(count):
            row = arrival[r]
            both = jnp.concatenate([state[row, 2 * g], state[row, 2 * g + 1]], axis=1)
            got = mm(lhs, both)
            from_k = jnp.where(row8 == r, got[0:8] + got[8:16], from_k)
            from_q = jnp.where(row8 == r, got[16:24] + got[24:32], from_q)
        pair = []
        for i in range(2):
            h = 2 * g + i
            s = carry[:, h : h + 1]
            v = stage[:, (v_at + h) * LANES : (v_at + h + 1) * LANES]
            z = stage[:, (g_at + h) * LANES : (g_at + h + 1) * LANES]
            delta = beta[:, h : h + 1] * (v - s * from_k[:, i * LANES : (i + 1) * LANES])
            o = s * from_q[:, i * LANES : (i + 1) * LANES] + qk * delta
            norm = lax.rsqrt(jnp.mean(o * o, axis=1, keepdims=True) + 1e-06)
            pair.append(o * norm * gain * silu(z))
        g_src[g * 16 : (g + 1) * 16, :] = jnp.concatenate(pair, axis=0).astype(BF16)

    for y in ys:
        send(g_src, g_in.at[my_y], 2, at_y(y))
    g_in[my_y] = g_src[...]

    whole_wait(r0_in.at[pl.ds(0, ny - 1)], recv_sem.at[0])
    ids = jnp.sum(r0_in[:, 0:PAD, :], axis=0)
    picks_w = jnp.sum(r0_in[:, PAD : 2 * PAD, :], axis=0)
    r1_src[...] = ids
    for zc in zcs:
        send(r1_src, r1_in.at[my_zc], 3, at_zc(zc))
    r1_in[my_zc] = ids

    sel_row = iota((32, LANES), 0)
    pick = jnp.bitwise_and(sel_row, 15)
    source = jnp.right_shift(sel_row, 4)
    sel = jnp.where(
        (iota((32, LANES), 1) == (SRC * my_x + source) * top + pick) & (pick < top), 1.0, 0.0
    ).astype(F32)
    spread = (iota((PAD, flat), 0) == jnp.bitwise_and(iota((PAD, flat), 1), 7)).astype(F32)
    flat_src = jnp.bitwise_and(jnp.right_shift(iota((16, flat), 1), 3), 1)

    def table(t):
        wide = mm(mm(sel, t, NT, EXACT), spread, precision=EXACT)
        return jnp.where(flat_src == 0, wide[0:16], wide[16:32])

    owner = jnp.floor((table(ids) - 1.0) * 0.5).astype(jnp.int32) - my_y * nzc
    weight = table(picks_w)
    zc_row = iota((nzc, flat), 0)
    hit = jnp.zeros((nzc, flat), F32)
    hit_w = jnp.zeros((nzc, flat), F32)
    for j in range(top):
        same = zc_row == owner[j : j + 1, :]
        hit = hit + jnp.where(same, 1.0, 0.0)
        hit_w = hit_w + jnp.where(same, weight[j : j + 1, :], 0.0)
    msg = SRC * chunks
    msg_row = iota((msg, flat), 0)
    msg_col = iota((msg, flat), 1)
    match = (
        jnp.bitwise_and(msg_row, chunks - 1) == jnp.right_shift(msg_col, 4)
    ) & (msg_row // chunks == jnp.bitwise_and(jnp.right_shift(msg_col, 3), 1))
    match = match.astype(F32)
    for zc in range(nzc):
        place[zc * msg : (zc + 1) * msg, :] = (hit[zc : zc + 1, :] * match).astype(BF16)
    weigh_t = hit_w.T
    hi = weigh_t.astype(BF16)
    lo = (weigh_t - hi.astype(F32)).astype(BF16)
    back = nzc * msg
    open_up = (iota((nzc, back), 0) == iota((nzc, back), 1) // msg).astype(BF16)
    w_row = iota((flat, back), 0)
    w_col = iota((flat, back), 1)
    kept = (jnp.right_shift(w_row, 4) == jnp.bitwise_and(w_col, chunks - 1)) & (
        jnp.bitwise_and(jnp.right_shift(w_row, 3), 1)
        == jnp.bitwise_and(w_col, msg - 1) // chunks
    )
    weigh[0] = jnp.where(kept, mm(hi, open_up), 0.0).astype(BF16)
    weigh[1] = jnp.where(kept, mm(lo, open_up), 0.0).astype(BF16)

    whole_wait(w_out.at[pl.ds(0, (nzc - 1) * 16), :], recv_sem.at[1])
    whole_wait(g_in.at[pl.ds(0, ny - 1)], recv_sem.at[2])
    first = jnp.zeros((ny * 16, nzc * 16), F32)
    second = jnp.zeros((ny * 16, nzc * 16), F32)
    for g in range(key_heads):
        rows = g_in[:, g * 16 : (g + 1) * 16, :].reshape(ny * 16, LANES)
        first += mm(rows, w_out[:, 2 * g * LANES : (2 * g + 1) * LANES], NT)
        second += mm(rows, w_out[:, (2 * g + 1) * LANES : (2 * g + 2) * LANES], NT)
    cols = nzc * 16
    part = first.reshape(ny, 2, PAD, cols)[:, 0] + second.reshape(ny, 2, PAD, cols)[:, 1]
    p_src[...] = part.reshape(nx, ROWS, cols)
    for x in xs:
        send(p_src.at[x], p_in.at[my_x], 4, at_x(x))
    p_in[my_x] = p_src[my_x]

    whole_wait(r1_in.at[pl.ds(0, nzc - 1)], recv_sem.at[3])
    slot = iota((nx * slots, nzc), 0)
    of_zc = jnp.right_shift(jnp.bitwise_and(slot, slots - 1), 1) == iota((nx * slots, nzc), 1)
    of_zc = of_zc.astype(BF16)
    slot = iota((nx * slots, LANES), 0)
    slot_y = SRC * (slot // slots) + jnp.bitwise_and(slot, 1)
    lane = iota((nx * slots, LANES), 1)
    of_y = (lane >= slot_y * top) & (lane < slot_y * top + top)
    arrived = r1_in[...]
    for e in range(2):
        named = (2 * ep + 1 + e).astype(F32)
        found = jnp.sum(jnp.where(arrived == named, 1.0, 0.0), axis=1).astype(BF16)
        found = jnp.where(of_y, mm(of_zc, found), 0.0)
        masks[e] = jnp.broadcast_to(jnp.sum(found, axis=1, keepdims=True), (nx * slots, LANES))

    whole_wait(p_in.at[pl.ds(0, nx - 1)], recv_sem.at[4])
    attn = p_in[0]
    for x in range(1, nx):
        attn = attn + p_in[x]
    attn = attn.astype(BF16).astype(F32)
    for i in range(y_chunks):
        base = jnp.concatenate(
            [r0_in[SRC * my_x + s, (2 + i) * PAD : (3 + i) * PAD, :] for s in range(SRC)], axis=0
        )
        c_src[i] = (base + attn[:, i * LANES : (i + 1) * LANES]).astype(BF16)
    for y in ys:
        send(c_src, c_in.at[my_y], 5, at_y(y))
    c_in[my_y] = c_src[...]
    whole_wait(c_in.at[pl.ds(0, ny - 1)], recv_sem.at[5])
    squares = jnp.zeros((ROWS, LANES), F32)
    for ch in range(chunks):
        c = c_in[ch // y_chunks, ch % y_chunks].astype(F32)
        squares = squares + c * c
    norm = lax.rsqrt(jnp.sum(squares, axis=1, keepdims=True) / width + 1e-06)
    for ch in range(chunks):
        c = c_in[ch // y_chunks, ch % y_chunks].astype(F32)
        n_scr[ch * 16 : (ch + 1) * 16, :] = (
            c * norm * ffn_gain[:, ch * LANES : (ch + 1) * LANES]
        ).astype(BF16)

    m3_src[...] = mm(place[...], n_scr[...]).astype(BF16).reshape(nzc, msg, LANES)
    for zc in zcs:
        send(m3_src.at[zc], m3_in.at[my_zc], 6, at_zc(zc))
    m3_in[my_zc] = m3_src[my_zc]
    turn_row = iota((flat, flat), 0)
    turn_col = iota((flat, flat), 1)
    unflat = (jnp.bitwise_and(turn_row, 15) == turn_col // chunks) & (
        jnp.right_shift(turn_row, 4) == jnp.bitwise_and(turn_col, chunks - 1)
    )
    unflat = unflat.astype(BF16)
    whole_wait(m3_in.at[pl.ds(0, nzc - 1)], recv_sem.at[6])
    for n in range(groups):
        block = mm(unflat, m3_in[n * 8 : (n + 1) * 8].reshape(flat, LANES)).astype(BF16)
        for ch in range(chunks):
            x_src[n * 16 : (n + 1) * 16, ch * LANES : (ch + 1) * LANES] = block[
                ch * 16 : (ch + 1) * 16
            ]
    for x in xs:
        send(x_src, x_in.at[my_x], 7, at_x(x))
    x_in[my_x] = x_src[...]

    for load in loads[1:]:
        load.wait()
    whole_wait(x_in.at[pl.ds(0, nx - 1)], recv_sem.at[7])
    rows = x_in[...].reshape(nx * slots, width)
    both = mm(rows, w_in[...])
    hidden = []
    for e in range(2):
        gate = both[:, e * LANES : (e + 1) * LANES]
        up = both[:, (2 + e) * LANES : (3 + e) * LANES]
        hidden.append(silu(gate) * up * masks[e])
    hidden = jnp.concatenate(hidden, axis=1).astype(BF16)
    result = mm(hidden, w_down[...]).reshape(nx, slots, width)
    y_own[...] = result
    y_src[...] = result.astype(BF16)
    for x in xs:
        send(y_src.at[x], y_in.at[my_x], 8, at_x(x))
    flatten = (jnp.bitwise_and(turn_col, 15) == turn_row // chunks) & (
        jnp.right_shift(turn_col, 4) == jnp.bitwise_and(turn_row, chunks - 1)
    )
    flatten = flatten.astype(BF16)
    y_in[my_x] = jnp.zeros_like(y_src[0])
    whole_wait(y_in.at[pl.ds(0, nx - 1)], recv_sem.at[8])

    for n in range(groups):
        tiles = []
        for ch in range(chunks):
            at = (pl.ds(n * 16, 16), pl.ds(ch * LANES, LANES))
            total = y_own[(my_x,) + at]
            for x in range(nx):
                total = total + y_in[(x,) + at].astype(F32)
            tiles.append(total.astype(BF16))
        block = mm(flatten, jnp.concatenate(tiles, axis=0)).astype(BF16)
        m6_src[n * 8 : (n + 1) * 8] = block.reshape(8, msg, LANES)
    for zc in zcs:
        send(m6_src.at[zc], m6_in.at[my_zc], 9, at_zc(zc))
    m6_in[my_zc] = m6_src[my_zc]
    whole_wait(m6_in.at[pl.ds(0, nzc - 1)], recv_sem.at[9])

    rows = m6_in[...].reshape(back, LANES)
    mixed = (mm(weigh[0], rows) + mm(weigh[1], rows)).reshape(chunks, ROWS, LANES)
    own_row = jnp.where(
        SRC * my_x + jnp.right_shift(iota((ROWS, LANES), 0), 3) == my_y, 1.0, 0.0
    ).astype(F32)
    for ch in range(chunks):
        c = c_in[ch // y_chunks, ch % y_chunks].astype(F32)
        m7_src[ch] = (mixed[ch] + c * own_row).reshape(SRC, PAD, LANES)
    for dx in range(nx):
        x = lax.rem(my_x + dx, nx)
        for s in range(SRC):
            y = SRC * my_x + s
            part = m7_src.at[pl.ds(x * x_chunks, x_chunks), s]
            if dx:
                send(part, m7_in.at[my_y], 10, (y * nzc + my_zc, x))
            else:
                keep = pltpu.make_async_copy(part, m7_in.at[my_y], recv_sem.at[10])
                away = pltpu.make_async_remote_copy(
                    src_ref=part,
                    dst_ref=m7_in.at[my_y],
                    send_sem=send_sem.at[10],
                    recv_sem=recv_sem.at[10],
                    device_id=(y * nzc + my_zc, x),
                    device_id_type=MESH,
                )

                @pl.when(y == my_y)
                def _():
                    keep.start()

                @pl.when(y != my_y)
                def _():
                    away.start()
                    away.wait_send()

    for copy in sent:
        copy.wait_send()
    whole_wait(m7_in, recv_sem.at[10])
    total = jnp.sum(m7_in[...], axis=0)
    for i in range(x_chunks):
        out[:, i * LANES : (i + 1) * LANES] = total[i, 0:count].astype(BF16)


def shards(
    nx,
    ny,
    nzc,
    residual_in,
    new_query,
    new_keys,
    new_values,
    out_gate,
    beta_logit,
    decay_logit,
    decay_base,
    decay_bias,
    norm_gain,
    state_store,
    state_scale,
    arrival,
    out_weight,
    ffn_gain,
    expert_gate_weight,
    expert_up_weight,
    expert_down_weight,
    route_ids,
    route_weight,
):
    count, width = residual_in.shape
    key_heads = new_query.shape[1] // LANES
    heads = 2 * key_heads
    top = route_ids.shape[1]
    chunks = width // LANES
    y_chunks = chunks // ny
    x_chunks = chunks // nx
    slots = nzc * SRC
    msg = SRC * chunks
    flat = 16 * chunks
    stage_tiles = 2 * key_heads + 2 * heads + chunks
    vmem = pl.BlockSpec(memory_space=pltpu.VMEM)
    smem = pl.BlockSpec(memory_space=pltpu.SMEM)
    anywhere = pl.BlockSpec(memory_space=pl.ANY)
    scratch = [
        pltpu.VMEM((PAD, stage_tiles * LANES), F32),
        pltpu.VMEM((4, PAD, LANES), F32),
        pltpu.VMEM(state_store.shape, BF16),
        pltpu.VMEM((width, 4 * LANES), BF16),
        pltpu.VMEM((2 * LANES, width), BF16),
        pltpu.VMEM((nzc * 16, heads * LANES), BF16),
        pltpu.VMEM((ny, (2 + y_chunks) * PAD, LANES), F32),
        pltpu.VMEM((ny, (2 + y_chunks) * PAD, LANES), F32),
        pltpu.VMEM((PAD, LANES), F32),
        pltpu.VMEM((nzc, PAD, LANES), F32),
        pltpu.VMEM((heads * PAD, LANES), BF16),
        pltpu.VMEM((ny, heads * PAD, LANES), BF16),
        pltpu.VMEM((nx, ROWS, nzc * 16), F32),
        pltpu.VMEM((nx, ROWS, nzc * 16), F32),
        pltpu.VMEM((y_chunks, ROWS, LANES), BF16),
        pltpu.VMEM((ny, y_chunks, ROWS, LANES), BF16),
        pltpu.VMEM((flat, LANES), BF16),
        pltpu.VMEM((nzc * msg, flat), BF16),
        pltpu.VMEM((2, flat, nzc * msg), BF16),
        pltpu.VMEM((2, nx * slots, LANES), F32),
        pltpu.VMEM((nzc, msg, LANES), BF16),
        pltpu.VMEM((nzc, msg, LANES), BF16),
        pltpu.VMEM((slots, width), BF16),
        pltpu.VMEM((nx, slots, width), BF16),
        pltpu.VMEM((nx, slots, width), F32),
        pltpu.VMEM((nx, slots, width), BF16),
        pltpu.VMEM((nx, slots, width), BF16),
        pltpu.VMEM((nzc, msg, LANES), BF16),
        pltpu.VMEM((nzc, msg, LANES), BF16),
        pltpu.VMEM((chunks, SRC, PAD, LANES), F32),
        pltpu.VMEM((ny, x_chunks, PAD, LANES), F32),
        pltpu.SemaphoreType.DMA((7,)),
        pltpu.SemaphoreType.DMA((11,)),
        pltpu.SemaphoreType.DMA((11,)),
    ]
    return pl.pallas_call(
        functools.partial(kernel, nx, ny, nzc, top),
        out_shape=jax.ShapeDtypeStruct((count, width // nx), BF16),
        in_specs=[vmem] * 11 + [smem] + [vmem] * 4 + [anywhere] * 4,
        out_specs=vmem,
        scratch_shapes=scratch,
        compiler_params=pltpu.CompilerParams(
            collective_id=0, has_side_effects=True, vmem_limit_bytes=40 * 1024 * 1024
        ),
        name="decode_layer",
    )(
        residual_in,
        new_query,
        new_keys,
        new_values,
        out_gate,
        beta_logit,
        decay_logit,
        decay_base[None, :],
        decay_bias[None, :],
        norm_gain[None, :],
        state_scale,
        arrival,
        out_weight,
        ffn_gain[None, :],
        route_ids,
        route_weight,
        state_store,
        expert_gate_weight,
        expert_up_weight,
        expert_down_weight,
    )


def solution(mesh):
    nx = mesh.shape["tp"]
    ny = SRC * nx
    nzc = mesh.shape["ep"] // ny
    return jax.shard_map(
        functools.partial(shards, nx, ny, nzc),
        mesh=mesh,
        in_specs=(
            P("ep", None),
            P("ep", "tp"),
            P("ep", "tp"),
            P("ep", "tp"),
            P("ep", "tp"),
            P("ep", "tp"),
            P("ep", "tp"),
            P("tp"),
            P("tp"),
            P(),
            P("ep", "tp", None, None),
            P("ep", "tp"),
            P("ep"),
            P("tp", "ep"),
            P(),
            P("ep", None, "tp"),
            P("ep", None, "tp"),
            P("ep", "tp", None),
            P("ep", None),
            P("ep", None),
        ),
        out_specs=P("ep", "tp"),
        check_vma=False,
    )
```

time: 258 us -> 97.9 us (0.38)
  the two profiles are of different devices: /device:TPU:1 before, /device:TPU:14 now
where the time goes in v1:
time: 97.9 us; the launch traced here: 97.1 us
  Pallas kernels  80.1 us (82%)
  local copies, waits for them, and re-layouts  16.9 us (17%)
    pallas_call x1, Pallas kernels, shards(): pl.pallas_call(functools.partial(kernel, nx, ny, nzc, top), out_shape=jax...  80.1 us
    unnamed x40, local copies, waits for them, and re-layouts  16.9 us

profile of v1, /device:TPU:14, one launch (start us, length us, event | category | flops | bytes accessed | tf_op | source)
XLA Modules:
  0.0 97.1 jit_solution(11483729447456429203)
XLA Ops:
  0.0 0.9 copy.21.out_weight
  0.9 0.0 copy-start
  0.9 1.4 %copy-done = bf16[6,8,128,128]{3,2,1,0:T(8,128)(2,1)S(1)} copy-done((bf16[6,8,128,128]{3,2,1,0:T(8,128)(2,1)S(1)}, bf16[6,8,128,128]{3,2,1,0:T(8,128)(2,1)}, u32[]{:S(2)}) %copy-start) | copy-done | bytes 1572888
  2.3 0.0 copy-start.1
  2.3 1.2 %copy-done.1 = bf16[2,2048,128]{2,1,0:T(8,128)(2,1)S(1)} copy-done((bf16[2,2048,128]{2,1,0:T(8,128)(2,1)S(1)}, bf16[2,2048,128]{2,1,0:T(8,128)(2,1)}, u32[]{:S(2)}) %copy-start.1) | copy-done | bytes 1048600
  3.6 0.0 copy-start.2
  3.6 1.2 %copy-done.2 = bf16[2,2048,128]{2,1,0:T(8,128)(2,1)S(1)} copy-done((bf16[2,2048,128]{2,1,0:T(8,128)(2,1)S(1)}, bf16[2,2048,128]{2,1,0:T(8,128)(2,1)}, u32[]{:S(2)}) %copy-start.2) | copy-done | bytes 1048600
  4.8 1.2 %copy-done.3 = bf16[2,128,2048]{2,1,0:T(8,128)(2,1)S(1)} copy-done((bf16[2,128,2048]{2,1,0:T(8,128)(2,1)S(1)}, bf16[2,128,2048]{2,1,0:T(8,128)(2,1)}, u32[]{:S(2)}) %copy-start.3) | copy-done | bytes 1048600
  6.0 0.0 copy-start.4
  6.0 0.8 copy-done.4
  6.8 0.0 copy-start.5
  6.8 0.7 copy-done.5
  7.5 0.0 copy-start.6
  7.5 0.7 copy-done.6
  8.2 0.0 copy-start.7
  8.2 0.7 copy-done.7
  8.9 0.0 copy-start.8
  8.9 0.7 copy-done.8
  9.6 0.0 copy-start.9
  9.6 0.7 copy-done.9
  10.3 0.0 copy-start.10
  10.3 0.7 copy-done.10
  11.0 0.7 copy-done.11
  11.7 0.7 copy-done.12
  12.4 0.7 copy-done.13
  13.1 0.7 copy-done.14
  13.7 0.7 copy-done.15
  14.4 0.7 copy-done.16
  15.1 0.7 copy-done.17
  15.7 0.7 copy-done.18
  16.4 80.1 %decode_layer.1 = bf16[6,512]{1,0:T(8,128)(2,1)S(1)} custom-call(bf16[6,2048]{1,0:T(8,128)(2,1)S(1)} %copy-done.4, bf16[6,512]{1,0:T(8,128)(2,1)S(1)} %copy-done.7, bf16[6,512]{1,0:T(8,128)(2,1)S(1)} %copy-done.8, bf16[6,1024]{1,0:T(8,128)(2,1)S(1)} %copy-done.5, bf16[6,1024]{1,0:T(8,128)(2,1)S(1)} %copy-done.6, f32[6,8]{1,0:T(8,128)S(1)} %copy-done.10, ...), custom_call_target="tpu_custom_call" | custom-call | tf_op jit(solution)/shard_map/decode_layer/pallas_call | solution.py:532
  96.5 0.6 copy.23
  (9 shorter events, 0.0 us)
Async XLA Ops:
  0.9 1.4 %copy-start = (bf16[6,8,128,128]{3,2,1,0:T(8,128)(2,1)S(1)}, bf16[6,8,128,128]{3,2,1,0:T(8,128)(2,1)}, u32[]{:S(2)}) copy-start(bf16[6,8,128,128]{3,2,1,0:T(8,128)(2,1)} %state_hbm.1) | copy-start | bytes 4718596
  2.3 1.2 %copy-start.1 = (bf16[2,2048,128]{2,1,0:T(8,128)(2,1)S(1)}, bf16[2,2048,128]{2,1,0:T(8,128)(2,1)}, u32[]{:S(2)}) copy-start(bf16[2,2048,128]{2,1,0:T(8,128)(2,1)} %gate_hbm.1) | copy-start | bytes 3145732
  3.6 1.2 %copy-start.2 = (bf16[2,2048,128]{2,1,0:T(8,128)(2,1)S(1)}, bf16[2,2048,128]{2,1,0:T(8,128)(2,1)}, u32[]{:S(2)}) copy-start(bf16[2,2048,128]{2,1,0:T(8,128)(2,1)} %up_hbm.1) | copy-start | bytes 3145732
  4.8 1.2 %copy-start.3 = (bf16[2,128,2048]{2,1,0:T(8,128)(2,1)S(1)}, bf16[2,128,2048]{2,1,0:T(8,128)(2,1)}, u32[]{:S(2)}) copy-start(bf16[2,128,2048]{2,1,0:T(8,128)(2,1)} %down_hbm.1) | copy-start | bytes 3145732
  6.0 0.8 copy-start.4
  6.8 0.7 copy-start.5
  7.5 0.7 copy-start.6
  8.2 0.7 copy-start.7
  8.9 0.7 copy-start.8
  9.6 0.7 copy-start.9
  10.3 0.7 copy-start.10
  11.0 0.7 copy-start.11
  11.7 0.7 copy-start.12
  12.4 0.7 copy-start.13
  13.1 0.7 copy-start.14
  13.7 0.7 copy-start.15
  14.4 0.7 copy-start.16
  15.1 0.7 copy-start.17
  15.7 0.7 copy-start.18

commit v2 on v1

v2 whole, which is shorter than its diff:
```python
import functools
import math

import jax
import jax.numpy as jnp
from jax import lax
from jax.experimental import pallas as pl
from jax.experimental.pallas import tpu as pltpu
from jax.sharding import PartitionSpec as P

MESH = pl.DeviceIdType.MESH
F32 = jnp.float32
BF16 = jnp.bfloat16
LANES = 128
PAD = 8
SRC = 2
ROWS = SRC * PAD
NT = (((1,), (1,)), ((), ()))
EXACT = lax.Precision.HIGHEST


def mm(a, b, dims=(((1,), (0,)), ((), ())), precision=None):
    return lax.dot_general(a, b, dims, preferred_element_type=F32, precision=precision)


def iota(shape, axis):
    return lax.broadcasted_iota(jnp.int32, shape, axis)


def silu(v):
    return v * jax.nn.sigmoid(v)


def whole_wait(ref, sem):
    pltpu.make_async_copy(ref, ref, sem).wait()


def kernel(
    nx,
    ny,
    nzc,
    top,
    residual_hbm,
    query_hbm,
    keys_hbm,
    values_hbm,
    out_gate_hbm,
    beta_logit_hbm,
    decay_logit_hbm,
    decay_base_hbm,
    decay_bias_hbm,
    norm_gain_hbm,
    state_scale_hbm,
    arrival_hbm,
    ffn_gain_hbm,
    route_ids_hbm,
    route_weight_hbm,
    out_weight_hbm,
    state_hbm,
    gate_hbm,
    up_hbm,
    down_hbm,
    out,
    residual,
    query,
    keys,
    values,
    out_gate,
    beta_logit,
    decay_logit,
    decay_base,
    decay_bias,
    norm_gain,
    state_scale,
    arrival,
    ffn_gain,
    route_ids,
    route_weight,
    stage,
    small,
    state,
    w_in,
    w_down,
    w_out,
    r0_src,
    r0_in,
    b_src,
    b_in,
    r1_src,
    r1_in,
    g_src,
    g_in,
    p_src,
    p_in,
    c_src,
    c_in,
    k_src,
    k_in,
    n_scr,
    place,
    weigh,
    masks,
    m3_src,
    m3_in,
    x_src,
    x_in,
    h_src,
    h_in,
    m6_src,
    m6_in,
    m7_own,
    m7_src,
    m7_in,
    small_sem,
    load_sem,
    send_sem,
    recv_sem,
):
    count, width = residual_hbm.shape
    chunks = width // LANES
    y_chunks = chunks // ny
    x_chunks = chunks // nx
    key_heads = query_hbm.shape[1] // LANES
    heads = 2 * key_heads
    nz = nzc // 2
    cols = nz * 16
    msg = SRC * chunks
    flat = 16 * chunks
    back = nzc * msg
    groups = nzc // 8
    block = nx * 16

    ep = lax.axis_index("ep")
    my_x = lax.axis_index("tp")
    my_y = ep // nzc
    my_zc = lax.rem(ep, nzc)
    my_z = my_zc // 2
    my_c = lax.rem(my_zc, 2)
    other = 1 - my_c

    def place_of(x, y, z, c):
        return (y * nzc + z * 2 + c, x)

    def at_zc(zc):
        return (my_y * nzc + zc, my_x)

    xs = [lax.rem(my_x + d, nx) for d in range(1, nx)]
    near_first = xs[0:1] + xs[2:] + xs[1:2]
    ys = [lax.rem(my_y + d, ny) for d in range(1, ny)]
    zs = [lax.rem(my_z + d, nz) for d in range(1, nz)]
    zcs = [lax.rem(my_zc + d, nzc) for d in range(1, nzc)]
    sibling = place_of(my_x, my_y, my_z, other)

    sent = []

    def remote(src, dst, hop, target):
        return pltpu.make_async_remote_copy(
            src_ref=src,
            dst_ref=dst,
            send_sem=send_sem.at[hop],
            recv_sem=recv_sem.at[hop],
            device_id=target,
            device_id_type=MESH,
        )

    def send(src, dst, hop, target):
        copy = remote(src, dst, hop, target)
        copy.start()
        sent.append(copy)

    own_cols = pl.ds(pl.multiple_of(my_z * 16, 16), 16)
    smalls = [
        pltpu.make_async_copy(src, dst, small_sem.at[n])
        for n, (src, dst) in enumerate(
            (
                (route_ids_hbm, route_ids),
                (route_weight_hbm, route_weight),
                (residual_hbm, residual),
                (query_hbm, query),
                (keys_hbm, keys),
                (values_hbm, values),
                (out_gate_hbm, out_gate),
                (beta_logit_hbm, beta_logit),
                (decay_logit_hbm, decay_logit),
                (decay_base_hbm, decay_base),
                (decay_bias_hbm, decay_bias),
                (norm_gain_hbm, norm_gain),
                (state_scale_hbm, state_scale),
                (arrival_hbm, arrival),
                (ffn_gain_hbm, ffn_gain),
            )
        )
    ]
    for load in smalls:
        load.start()
    state_load = pltpu.make_async_copy(state_hbm, state, load_sem.at[0])
    state_load.start()
    w_own = pltpu.make_async_copy(out_weight_hbm, w_out.at[own_cols, :], load_sem.at[1])
    w_own.start()

    barrier = pltpu.get_barrier_semaphore()
    peers = [at_zc(zc) for zc in zcs]
    for c in (my_c, other):
        peers += [place_of(my_x, y, my_z, c) for y in ys]
        peers += [place_of(x, my_y, my_z, c) for x in xs]
    for peer in peers:
        pl.semaphore_signal(barrier, inc=1, device_id=peer, device_id_type=MESH)
    pl.semaphore_wait(barrier, len(peers))

    for z in zs:
        send(out_weight_hbm, w_out.at[own_cols, :], 1, place_of(my_x, my_y, z, my_c))

    x_width = x_chunks * LANES
    for x in near_first[0:2]:
        span = pl.ds(pl.multiple_of(x * x_width, x_width), x_width)
        send(down_hbm.at[:, :, span], w_down.at[my_x], 15, place_of(x, my_y, my_z, my_c))

    stage[...] = jnp.zeros_like(stage)
    small[...] = jnp.zeros_like(small)
    q_at, k_at, v_at, g_at = 0, key_heads, 2 * key_heads, 2 * key_heads + heads
    r_at = g_at + heads
    for load in smalls:
        load.wait()
    for at, ref in ((q_at, query), (k_at, keys), (v_at, values), (g_at, out_gate)):
        stage[0:count, at * LANES : at * LANES + ref.shape[1]] = ref[...].astype(F32)
    small[2, 0:count, 0:heads] = decay_logit[...]
    small[3, 0:count, 0:heads] = beta_logit[...]
    rate = jnp.exp(decay_base[...])
    logit = small[2, :, 0:heads] + decay_bias[...]
    soft = jnp.maximum(logit, 0.0) + jnp.log1p(jnp.exp(-jnp.abs(logit)))
    decay = jnp.exp(-rate * soft)
    beta = jax.nn.sigmoid(small[3, :, 0:heads])
    row8 = iota((PAD, 1), 0)
    moved = jnp.zeros((PAD, heads), F32)
    for r in range(count):
        moved = jnp.where(row8 == r, state_scale[pl.ds(arrival[r], 1), :], moved)
    carry = moved * decay
    gain = norm_gain[...]
    state_load.wait()
    for g in range(key_heads):
        q = stage[:, (q_at + g) * LANES : (q_at + g + 1) * LANES]
        k = stage[:, (k_at + g) * LANES : (k_at + g + 1) * LANES]
        q = q * (lax.rsqrt(jnp.sum(q * q, axis=1, keepdims=True) + 1e-06) / math.sqrt(LANES))
        k = k * lax.rsqrt(jnp.sum(k * k, axis=1, keepdims=True) + 1e-06)
        qk = jnp.sum(q * k, axis=1, keepdims=True)
        k_hi = k.astype(BF16).astype(F32)
        q_hi = q.astype(BF16).astype(F32)
        lhs = jnp.concatenate([k_hi, k - k_hi, q_hi, q - q_hi], axis=0).astype(BF16)
        from_k = jnp.zeros((PAD, 2 * LANES), F32)
        from_q = jnp.zeros((PAD, 2 * LANES), F32)
        for r in range(count):
            row = arrival[r]
            both = jnp.concatenate([state[row, 2 * g], state[row, 2 * g + 1]], axis=1)
            got = mm(lhs, both)
            from_k = jnp.where(row8 == r, got[0:8] + got[8:16], from_k)
            from_q = jnp.where(row8 == r, got[16:24] + got[24:32], from_q)
        pair = []
        for i in range(2):
            h = 2 * g + i
            s = carry[:, h : h + 1]
            v = stage[:, (v_at + h) * LANES : (v_at + h + 1) * LANES]
            z = stage[:, (g_at + h) * LANES : (g_at + h + 1) * LANES]
            delta = beta[:, h : h + 1] * (v - s * from_k[:, i * LANES : (i + 1) * LANES])
            o = s * from_q[:, i * LANES : (i + 1) * LANES] + qk * delta
            norm = lax.rsqrt(jnp.mean(o * o, axis=1, keepdims=True) + 1e-06)
            pair.append(o * norm * gain * silu(z))
        g_src[g * 16 : (g + 1) * 16, :] = jnp.concatenate(pair, axis=0).astype(BF16)
    for y in ys:
        for c in (my_c, other):
            send(g_src, g_in.at[my_c * ny + my_y], 2, place_of(my_x, y, my_z, c))
    send(g_src, g_in.at[my_c * ny + my_y], 2, sibling)
    g_in[my_c * ny + my_y] = g_src[...]

    small[0, 0:count, 0:top] = (route_ids[...] + 1).astype(F32)
    small[1, 0:count, 0:top] = route_weight[...]
    r0_src[...] = small[0] + pltpu.roll(small[1], LANES // 2, 1)
    stage[0:count, r_at * LANES : r_at * LANES + width] = residual[...].astype(F32)
    for y in range(ny):
        at = (r_at + y * y_chunks) * LANES
        tiles = [stage[:, at + i * LANES : at + (i + 1) * LANES] for i in range(y_chunks)]
        b_src[y] = jnp.concatenate(tiles, axis=0).astype(BF16)
    for y in ys:
        send(r0_src, r0_in.at[my_y], 0, place_of(my_x, y, my_z, my_c))
        send(b_src.at[y], b_in.at[my_y], 16, place_of(my_x, y, my_z, my_c))
    r0_in[my_y] = r0_src[...]
    b_in[my_y] = b_src[my_y]

    w_loads = []
    for e in range(2):
        for n, ref in ((0, gate_hbm), (2, up_hbm)):
            w_loads.append(
                pltpu.make_async_copy(
                    ref.at[e], w_in.at[:, pl.ds((n + e) * LANES, LANES)], load_sem.at[2 + n + e]
                )
            )
    own_width = pl.ds(pl.multiple_of(my_x * x_width, x_width), x_width)
    w_loads.append(
        pltpu.make_async_copy(down_hbm.at[:, :, own_width], w_down.at[my_x], load_sem.at[6])
    )
    for load in w_loads:
        load.start()

    w_own.wait()
    whole_wait(w_out.at[pl.ds(0, (nz - 1) * 16), :], recv_sem.at[1])
    whole_wait(g_in.at[pl.ds(0, 2 * ny - 1)], recv_sem.at[2])
    first = jnp.zeros((2 * ny * 16, cols), F32)
    second = jnp.zeros((2 * ny * 16, cols), F32)
    for g in range(key_heads):
        rows = g_in[:, g * 16 : (g + 1) * 16, :].reshape(2 * ny * 16, LANES)
        first += mm(rows, w_out[:, 2 * g * LANES : (2 * g + 1) * LANES], NT)
        second += mm(rows, w_out[:, (2 * g + 1) * LANES : (2 * g + 2) * LANES], NT)
    part = first.reshape(2 * ny, 2, PAD, cols)[:, 0] + second.reshape(2 * ny, 2, PAD, cols)[:, 1]
    p_src[...] = part.reshape(2, nx, ROWS, cols)
    for x in xs:
        for c in (my_c, other):
            send(p_src.at[c, x], p_in.at[my_c * nx + my_x], 4, place_of(x, my_y, my_z, c))
    send(p_src.at[other, my_x], p_in.at[my_c * nx + my_x], 4, sibling)
    p_in[my_c * nx + my_x] = p_src[my_c, my_x]
    span = pl.ds(pl.multiple_of(xs[1] * x_width, x_width), x_width)
    send(down_hbm.at[:, :, span], w_down.at[my_x], 15, place_of(xs[1], my_y, my_z, my_c))

    whole_wait(r0_in.at[pl.ds(0, ny - 1)], recv_sem.at[0])
    low = iota((PAD, LANES), 1) < LANES // 2
    ids = jnp.zeros((PAD, LANES), F32)
    picks_w = jnp.zeros((PAD, LANES), F32)
    for y in range(ny):
        both = r0_in[y]
        ids = ids + pltpu.roll(jnp.where(low, both, 0.0), y * top, 1)
        picks_w = picks_w + pltpu.roll(
            jnp.where(low, 0.0, both), (y * top + LANES // 2) % LANES, 1
        )
    r1_src[...] = ids
    for zc in zcs:
        send(r1_src, r1_in.at[my_zc], 3, at_zc(zc))
    r1_in[my_zc] = ids

    def owner_of(t):
        return jnp.floor((t - 1.0) * 0.5).astype(jnp.int32) - my_y * nzc

    sel_row = iota((32, LANES), 0)
    pick = jnp.bitwise_and(sel_row, 15)
    source = SRC * my_x + jnp.right_shift(sel_row, 4)
    sel = ((iota((32, LANES), 1) == source * top + pick) & (pick < top)).astype(F32)
    spread = (iota((PAD, flat), 0) == jnp.bitwise_and(iota((PAD, flat), 1), 7)).astype(F32)
    flat_src = jnp.bitwise_and(jnp.right_shift(iota((16, flat), 1), 3), 1)
    wide = mm(mm(sel, ids, NT, EXACT), spread, precision=EXACT)
    owner = owner_of(jnp.where(flat_src == 0, wide[0:16], wide[16:32]))
    zc_row = iota((nzc, flat), 0)
    hit = jnp.zeros((nzc, flat), F32)
    for j in range(top):
        hit = hit + jnp.where(zc_row == owner[j : j + 1, :], 1.0, 0.0)
    msg_row = iota((msg, flat), 0)
    msg_col = iota((msg, flat), 1)
    match = (jnp.bitwise_and(msg_row, chunks - 1) == jnp.right_shift(msg_col, 4)) & (
        msg_row // chunks == jnp.bitwise_and(jnp.right_shift(msg_col, 3), 1)
    )
    match = match.astype(F32)
    for zc in range(nzc):
        place[zc * msg : (zc + 1) * msg, :] = (hit[zc : zc + 1, :] * match).astype(BF16)

    mixed_rows = ny * x_chunks * PAD
    sel_row = iota((ny * 16, LANES), 0)
    pick = jnp.bitwise_and(sel_row, 15)
    source = jnp.right_shift(sel_row, 4)
    sel = ((iota((ny * 16, LANES), 1) == source * top + pick) & (pick < top)).astype(F32)
    spread = (
        iota((PAD, mixed_rows), 0) == jnp.bitwise_and(iota((PAD, mixed_rows), 1), 7)
    ).astype(F32)
    of_source = iota((16, mixed_rows), 1) // (x_chunks * PAD)

    def table(t):
        wide = mm(mm(sel, t, NT, EXACT), spread, precision=EXACT)
        kept = jnp.zeros((16, mixed_rows), F32)
        for y in range(ny):
            kept = jnp.where(of_source == y, wide[y * 16 : (y + 1) * 16], kept)
        return kept

    owner = owner_of(table(ids))
    weight = table(picks_w)
    zc_row = iota((nzc, mixed_rows), 0)
    hit_w = jnp.zeros((nzc, mixed_rows), F32)
    for j in range(top):
        hit_w = hit_w + jnp.where(zc_row == owner[j : j + 1, :], weight[j : j + 1, :], 0.0)
    weigh_t = hit_w.T
    hi = weigh_t.astype(BF16)
    lo = (weigh_t - hi.astype(F32)).astype(BF16)
    open_up = (iota((nzc, back), 0) == iota((nzc, back), 1) // msg).astype(BF16)
    w_row = iota((mixed_rows, back), 0)
    w_col = iota((mixed_rows, back), 1)
    kept = jnp.right_shift(w_row, 3) == jnp.bitwise_and(w_col, msg - 1)
    weigh[0] = jnp.where(kept, mm(hi, open_up), 0.0).astype(BF16)
    weigh[1] = jnp.where(kept, mm(lo, open_up), 0.0).astype(BF16)

    mix_row = iota((2 * cols, 2 * cols), 0)
    mix_col = iota((2 * cols, 2 * cols), 1)
    mix = (
        (mix_row // cols == jnp.bitwise_and(jnp.right_shift(mix_col, 4), 1))
        & (
            jnp.right_shift(jnp.bitwise_and(mix_row, cols - 1), 4)
            == jnp.right_shift(mix_col, 5)
        )
        & (jnp.bitwise_and(mix_row, 15) == jnp.bitwise_and(mix_col, 15))
    )
    mix = mix.astype(BF16)

    whole_wait(b_in.at[pl.ds(0, ny - 1)], recv_sem.at[16])
    whole_wait(p_in.at[pl.ds(0, 2 * nx - 1)], recv_sem.at[4])
    attn = []
    for c in range(2):
        total = p_in[c * nx]
        for x in range(1, nx):
            total = total + p_in[c * nx + x]
        attn.append(total.astype(BF16))
    attn = mm(jnp.concatenate(attn, axis=1), mix)
    base_rows = [b_in[SRC * my_x + s].astype(F32) for s in range(SRC)]
    for i in range(y_chunks):
        base = jnp.concatenate([rows[i * PAD : (i + 1) * PAD] for rows in base_rows], axis=0)
        c_src[i] = (base + attn[:, i * LANES : (i + 1) * LANES]).astype(BF16)
    for y in ys:
        send(c_src, c_in.at[my_y], 5, place_of(my_x, y, my_z, my_c))
    c_in[my_y] = c_src[...]

    whole_wait(r1_in.at[pl.ds(0, nzc - 1)], recv_sem.at[3])
    slot = iota((groups * block, nzc), 0)
    slot_zc = (slot // block) * 8 + jnp.bitwise_and(jnp.right_shift(slot, 1), 7)
    of_zc = (slot_zc == iota((groups * block, nzc), 1)).astype(BF16)
    slot = iota((groups * block, LANES), 0)
    slot_x = jnp.right_shift(jnp.bitwise_and(slot, block - 1), 4)
    slot_y = SRC * slot_x + jnp.bitwise_and(slot, 1)
    lane = iota((groups * block, LANES), 1)
    of_y = (lane >= slot_y * top) & (lane < slot_y * top + top)
    arrived = r1_in[...]
    for e in range(2):
        named = (2 * ep + 1 + e).astype(F32)
        found = jnp.sum(jnp.where(arrived == named, 1.0, 0.0), axis=1).astype(BF16)
        found = jnp.where(of_y, mm(of_zc, found), 0.0)
        masks[e] = jnp.broadcast_to(
            jnp.sum(found, axis=1, keepdims=True), (groups * block, LANES)
        )

    whole_wait(c_in.at[pl.ds(0, ny - 1)], recv_sem.at[5])
    squares = jnp.zeros((ROWS, LANES), F32)
    for ch in range(chunks):
        c = c_in[ch // y_chunks, ch % y_chunks].astype(F32)
        squares = squares + c * c
    norm = lax.rsqrt(jnp.sum(squares, axis=1, keepdims=True) / width + 1e-06)
    for ch in range(chunks):
        c = c_in[ch // y_chunks, ch % y_chunks].astype(F32)
        n_scr[ch * 16 : (ch + 1) * 16, :] = (
            c * norm * ffn_gain[:, ch * LANES : (ch + 1) * LANES]
        ).astype(BF16)

    m3_src[...] = mm(place[...], n_scr[...]).astype(BF16).reshape(nzc, msg, LANES)
    my_group = my_zc // 8
    for zc in zcs:
        send(m3_src.at[zc], m3_in.at[my_zc], 6 + my_group, at_zc(zc))
    m3_own = pltpu.make_async_copy(m3_src.at[my_zc], m3_in.at[my_zc], recv_sem.at[6 + my_group])
    m3_own.start()

    half = my_y - SRC * my_x
    home = (half >= 0) & (half < SRC)
    for x in range(nx):
        tiles = []
        for ch in range(x * x_chunks, (x + 1) * x_chunks):
            c = c_in[ch // y_chunks, ch % y_chunks].astype(F32)
            tiles.append(jnp.where(half == 0, c[0:PAD], c[PAD : 2 * PAD]))
        k_src[x] = jnp.concatenate(tiles, axis=0).astype(BF16)
    k_away = [remote(k_src.at[x], k_in, 14, place_of(x, my_y, my_z, my_c)) for x in xs]
    k_own = pltpu.make_async_copy(k_src.at[my_x], k_in, recv_sem.at[14])

    @pl.when(home)
    def _():
        k_own.start()
        for copy in k_away:
            copy.start()

    turn_row = iota((flat, flat), 0)
    turn_col = iota((flat, flat), 1)
    unflat = (jnp.bitwise_and(turn_row, 15) == turn_col // chunks) & (
        jnp.right_shift(turn_row, 4) == jnp.bitwise_and(turn_col, chunks - 1)
    )
    unflat = unflat.astype(BF16)
    for n in range(groups):
        whole_wait(m3_in.at[pl.ds(n * 8, 8)], recv_sem.at[6 + n])
        turned = mm(unflat, m3_in[n * 8 : (n + 1) * 8].reshape(flat, LANES)).astype(BF16)
        for ch in range(chunks):
            x_src[n, :, ch * LANES : (ch + 1) * LANES] = turned[ch * 16 : (ch + 1) * 16]
        for x in near_first:
            send(x_src.at[n], x_in.at[n, my_x], 8 + n, place_of(x, my_y, my_z, my_c))
        x_in[n, my_x] = x_src[n]

    for load in w_loads:
        load.wait()
    for n in range(groups):
        whole_wait(x_in.at[n, pl.ds(0, nx - 1)], recv_sem.at[8 + n])
        both = mm(x_in[n].reshape(block, width), w_in[...])
        hidden = jnp.zeros((block, LANES), F32)
        for e in range(2):
            gate = both[:, e * LANES : (e + 1) * LANES]
            up = both[:, (2 + e) * LANES : (3 + e) * LANES]
            hidden = hidden + silu(gate) * up * masks[e, n * block : (n + 1) * block]
        h_src[n] = hidden.astype(BF16)
        for x in xs:
            send(h_src.at[n], h_in.at[n, my_x], 10 + n, place_of(x, my_y, my_z, my_c))
        h_in[n, my_x] = h_src[n]

    back_row = iota((block * x_chunks, block * x_chunks), 0)
    back_col = iota((block * x_chunks, block * x_chunks), 1)
    row_y = (back_row % msg) // x_chunks
    slot = jnp.bitwise_and(back_col, 15)
    flatten = (
        (back_row // msg == jnp.right_shift(slot, 1))
        & (row_y == SRC * (back_col // (16 * x_chunks)) + jnp.bitwise_and(slot, 1))
        & (back_row % x_chunks == jnp.right_shift(back_col, 4) % x_chunks)
    )
    flatten = flatten.astype(BF16)
    whole_wait(w_down.at[pl.ds(0, nx - 1)], recv_sem.at[15])
    for n in range(groups):
        whole_wait(h_in.at[n, pl.ds(0, nx - 1)], recv_sem.at[10 + n])
        total = jnp.zeros((block, x_width), F32)
        for x in range(nx):
            h = h_in[n, x].astype(F32)
            for e in range(2):
                chosen = (h * masks[e, n * block : (n + 1) * block]).astype(BF16)
                total = total + mm(chosen, w_down[x, e])
        total = total.astype(BF16)
        tiles = [
            total[x * 16 : (x + 1) * 16, ch * LANES : (ch + 1) * LANES]
            for x in range(nx)
            for ch in range(x_chunks)
        ]
        turned = mm(flatten, jnp.concatenate(tiles, axis=0)).astype(BF16)
        m6_src[n * 8 : (n + 1) * 8] = turned.reshape(8, msg, LANES)
        for i in range(8):
            zc = n * 8 + i
            away = remote(m6_src.at[zc], m6_in.at[my_zc], 12, at_zc(zc))
            keep = pltpu.make_async_copy(m6_src.at[zc], m6_in.at[my_zc], recv_sem.at[12])

            @pl.when(zc == my_zc)
            def _():
                keep.start()

            @pl.when(zc != my_zc)
            def _():
                away.start()

    whole_wait(m6_in, recv_sem.at[12])
    rows = m6_in[...].reshape(back, LANES)
    mixed = (mm(weigh[0], rows) + mm(weigh[1], rows)).reshape(ny, x_chunks * PAD, LANES)
    m7_own[...] = mixed
    m7_src[...] = mixed.astype(BF16)
    for y in ys:
        send(m7_src.at[y], m7_in.at[my_y], 13, place_of(my_x, y, my_z, my_c))

    for copy in sent:
        copy.wait_send()
    whole_wait(m6_src.at[pl.ds(0, nzc - 1)], send_sem.at[12])

    @pl.when(home)
    def _():
        for copy in k_away:
            copy.wait_send()

    whole_wait(k_in, recv_sem.at[14])
    whole_wait(m7_in.at[pl.ds(0, ny - 1)], recv_sem.at[13])
    total = m7_own[my_y]
    for y in ys:
        total = total + m7_in[y].astype(F32)
    total = (total + k_in[...].astype(F32)).reshape(x_chunks, PAD, LANES)
    for i in range(x_chunks):
        out[:, i * LANES : (i + 1) * LANES] = total[i, 0:count].astype(BF16)


def shards(
    nx,
    ny,
    nzc,
    residual_in,
    new_query,
    new_keys,
    new_values,
    out_gate,
    beta_logit,
    decay_logit,
    decay_base,
    decay_bias,
    norm_gain,
    state_store,
    state_scale,
    arrival,
    out_weight,
    ffn_gain,
    expert_gate_weight,
    expert_up_weight,
    expert_down_weight,
    route_ids,
    route_weight,
):
    count, width = residual_in.shape
    key_heads = new_query.shape[1] // LANES
    heads = 2 * key_heads
    top = route_ids.shape[1]
    chunks = width // LANES
    y_chunks = chunks // ny
    x_chunks = chunks // nx
    msg = SRC * chunks
    flat = 16 * chunks
    cols = nzc // 2 * 16
    groups = nzc // 8
    block = nx * 16
    stage_tiles = 2 * key_heads + 2 * heads + chunks
    vmem = pl.BlockSpec(memory_space=pltpu.VMEM)
    hbm = pl.BlockSpec(memory_space=pltpu.HBM)
    small_operands = (
        residual_in,
        new_query,
        new_keys,
        new_values,
        out_gate,
        beta_logit,
        decay_logit,
        decay_base[None, :],
        decay_bias[None, :],
        norm_gain[None, :],
        state_scale,
        arrival,
        ffn_gain[None, :],
        route_ids,
        route_weight,
    )
    scratch = [
        (pltpu.SMEM if a is arrival else pltpu.VMEM)(a.shape, a.dtype) for a in small_operands
    ] + [
        pltpu.VMEM((PAD, stage_tiles * LANES), F32),
        pltpu.VMEM((4, PAD, LANES), F32),
        pltpu.VMEM(state_store.shape, BF16),
        pltpu.VMEM((width, 4 * LANES), BF16),
        pltpu.VMEM((nx, 2, LANES, width // nx), BF16),
        pltpu.VMEM((cols, heads * LANES), BF16),
        pltpu.VMEM((PAD, LANES), F32),
        pltpu.VMEM((ny, PAD, LANES), F32),
        pltpu.VMEM((ny, y_chunks * PAD, LANES), BF16),
        pltpu.VMEM((ny, y_chunks * PAD, LANES), BF16),
        pltpu.VMEM((PAD, LANES), F32),
        pltpu.VMEM((nzc, PAD, LANES), F32),
        pltpu.VMEM((heads * PAD, LANES), BF16),
        pltpu.VMEM((2 * ny, heads * PAD, LANES), BF16),
        pltpu.VMEM((2, nx, ROWS, cols), F32),
        pltpu.VMEM((2 * nx, ROWS, cols), F32),
        pltpu.VMEM((y_chunks, ROWS, LANES), BF16),
        pltpu.VMEM((ny, y_chunks, ROWS, LANES), BF16),
        pltpu.VMEM((nx, x_chunks * PAD, LANES), BF16),
        pltpu.VMEM((x_chunks * PAD, LANES), BF16),
        pltpu.VMEM((flat, LANES), BF16),
        pltpu.VMEM((nzc * msg, flat), BF16),
        pltpu.VMEM((2, ny * x_chunks * PAD, nzc * msg), BF16),
        pltpu.VMEM((2, groups * block, LANES), F32),
        pltpu.VMEM((nzc, msg, LANES), BF16),
        pltpu.VMEM((nzc, msg, LANES), BF16),
        pltpu.VMEM((groups, 16, width), BF16),
        pltpu.VMEM((groups, nx, 16, width), BF16),
        pltpu.VMEM((groups, block, LANES), BF16),
        pltpu.VMEM((groups, nx, block, LANES), BF16),
        pltpu.VMEM((nzc, msg, LANES), BF16),
        pltpu.VMEM((nzc, msg, LANES), BF16),
        pltpu.VMEM((ny, x_chunks * PAD, LANES), F32),
        pltpu.VMEM((ny, x_chunks * PAD, LANES), BF16),
        pltpu.VMEM((ny, x_chunks * PAD, LANES), BF16),
        pltpu.SemaphoreType.DMA((len(small_operands),)),
        pltpu.SemaphoreType.DMA((8,)),
        pltpu.SemaphoreType.DMA((17,)),
        pltpu.SemaphoreType.DMA((17,)),
    ]
    return pl.pallas_call(
        functools.partial(kernel, nx, ny, nzc, top),
        out_shape=jax.ShapeDtypeStruct((count, width // nx), BF16),
        in_specs=[hbm] * (len(small_operands) + 5),
        out_specs=vmem,
        scratch_shapes=scratch,
        compiler_params=pltpu.CompilerParams(
            collective_id=0, has_side_effects=True, vmem_limit_bytes=60 * 1024 * 1024
        ),
        name="decode_layer",
    )(
        *small_operands,
        out_weight.T,
        state_store,
        expert_gate_weight,
        expert_up_weight,
        expert_down_weight,
    )


def solution(mesh):
    nx = mesh.shape["tp"]
    ny = SRC * nx
    nzc = mesh.shape["ep"] // ny
    return jax.shard_map(
        functools.partial(shards, nx, ny, nzc),
        mesh=mesh,
        in_specs=(
            P("ep", None),
            P("ep", "tp"),
            P("ep", "tp"),
            P("ep", "tp"),
            P("ep", "tp"),
            P("ep", "tp"),
            P("ep", "tp"),
            P("tp"),
            P("tp"),
            P(),
            P("ep", "tp", None, None),
            P("ep", "tp"),
            P("ep"),
            P("tp", "ep"),
            P(),
            P("ep", None, "tp"),
            P("ep", None, "tp"),
            P("ep", "tp", None),
            P("ep", None),
            P("ep", None),
        ),
        out_specs=P("ep", "tp"),
        check_vma=False,
    )
```

time: 97.9 us -> 62.9 us (0.64)
  the two profiles are of different devices: /device:TPU:14 before, /device:TPU:1 now
where the time goes in v2:
time: 62.9 us; the launch traced here: 62.8 us
  Pallas kernels  61.5 us (98%)
  local copies, waits for them, and re-layouts  1.3 us (2%)
    pallas_call x1, Pallas kernels, shards(): pl.pallas_call(functools.partial(kernel, nx, ny, nzc, top), out_shape=jax...  61.5 us
    unnamed x1, local copies, waits for them, and re-layouts  1.3 us

profile of v2, /device:TPU:1, one launch (start us, length us, event | category | flops | bytes accessed | tf_op | source)
XLA Modules:
  0.0 62.8 jit_solution(17880041298845411994)
XLA Ops:
  0.0 61.5 %decode_layer.1 = bf16[6,512]{1,0:T(8,128)(2,1)} custom-call(bf16[6,2048]{1,0:T(8,128)(2,1)} %residual_hbm.1, bf16[6,512]{1,0:T(8,128)(2,1)} %query_hbm.1, bf16[6,512]{1,0:T(8,128)(2,1)} %keys_hbm.1, bf16[6,1024]{1,0:T(8,128)(2,1)} %values_hbm.1, bf16[6,1024]{1,0:T(8,128)(2,1)} %out_gate_hbm.1, f32[6,8]{1,0:T(8,128)} %beta_logit_hbm.1, ...), custom_call_target="tpu_custom_call" | custom-call | tf_op jit(solution)/shard_map/decode_layer/pallas_call | solution.py:674
  61.5 1.3 %copy.22 = bf16[6,512]{1,0:T(8,128)(2,1)} copy(bf16[6,512]{1,0:T(8,128)(2,1)} %decode_layer.1) | data formatting | bytes 12288

commit v3 on v2

--- a/solution.py
+++ b/solution.py
@@ -14,6 +14,8 @@
 LANES = 128
 PAD = 8
 SRC = 2
+Z_ORDER = (0, 1, 7, 2, 6, 3, 5, 4)
+Y_ORDER = (4, 3, 5, 2, 6, 1, 7, 0)
 ROWS = SRC * PAD
 NT = (((1,), (1,)), ((), ()))
 EXACT = lax.Precision.HIGHEST
@@ -88,15 +90,14 @@
     b_in,
     r1_src,
     r1_in,
+    g_pad,
     g_src,
     g_in,
+    g_all,
     p_src,
     p_in,
-    c_src,
-    c_in,
     k_src,
     k_in,
-    n_scr,
     place,
     weigh,
     masks,
@@ -108,9 +109,6 @@
     h_in,
     m6_src,
     m6_in,
-    m7_own,
-    m7_src,
-    m7_in,
     small_sem,
     load_sem,
     send_sem,
@@ -126,7 +124,8 @@
     cols = nz * 16
     msg = SRC * chunks
     flat = 16 * chunks
-    back = nzc * msg
+    owners = ny * nzc
+    back = owners * 4
     groups = nzc // 8
     block = nx * 16
 
@@ -150,6 +149,10 @@
     zs = [lax.rem(my_z + d, nz) for d in range(1, nz)]
     zcs = [lax.rem(my_zc + d, nzc) for d in range(1, nzc)]
     sibling = place_of(my_x, my_y, my_z, other)
+
+    order = Z_ORDER
+    z_from = [lax.rem(my_z + d, nz) for d in order]
+    z_to = [lax.rem(my_z + nz - d, nz) for d in order]
 
     sent = []
 
@@ -264,7 +267,12 @@
             o = s * from_q[:, i * LANES : (i + 1) * LANES] + qk * delta
             norm = lax.rsqrt(jnp.mean(o * o, axis=1, keepdims=True) + 1e-06)
             pair.append(o * norm * gain * silu(z))
-        g_src[g * 16 : (g + 1) * 16, :] = jnp.concatenate(pair, axis=0).astype(BF16)
+        g_pad[g * 16 : (g + 1) * 16, :] = jnp.concatenate(pair, axis=0).astype(BF16)
+    row = iota((count * heads, heads * PAD), 0)
+    col = iota((count * heads, heads * PAD), 1)
+    filled = jnp.bitwise_and(col, 7) < count
+    pack = (row == jnp.right_shift(col, 3) * count + jnp.bitwise_and(col, 7)) & filled
+    g_src[...] = mm(pack.astype(BF16), g_pad[...]).astype(BF16)
     for y in ys:
         for c in (my_c, other):
             send(g_src, g_in.at[my_c * ny + my_y], 2, place_of(my_x, y, my_z, c))
@@ -273,7 +281,7 @@
 
     small[0, 0:count, 0:top] = (route_ids[...] + 1).astype(F32)
     small[1, 0:count, 0:top] = route_weight[...]
-    r0_src[...] = small[0] + pltpu.roll(small[1], LANES // 2, 1)
+    r0_src[...] = pltpu.roll(small[0], my_y * top, 1)
     stage[0:count, r_at * LANES : r_at * LANES + width] = residual[...].astype(F32)
     for y in range(ny):
         at = (r_at + y * y_chunks) * LANES
@@ -302,11 +310,19 @@
 
     w_own.wait()
     whole_wait(w_out.at[pl.ds(0, (nz - 1) * 16), :], recv_sem.at[1])
+    row = iota((4 * heads * PAD, 4 * heads * count), 0)
+    col = iota((4 * heads * PAD, 4 * heads * count), 1)
+    filled = jnp.bitwise_and(row, 7) < count
+    unpack = (col == jnp.right_shift(row, 3) * count + jnp.bitwise_and(row, 7)) & filled
+    unpack = unpack.astype(BF16)
     whole_wait(g_in.at[pl.ds(0, 2 * ny - 1)], recv_sem.at[2])
+    for n in range(0, 2 * ny, 4):
+        four = mm(unpack, g_in[n : n + 4].reshape(4 * heads * count, LANES))
+        g_all[n : n + 4] = four.astype(BF16).reshape(4, heads * PAD, LANES)
     first = jnp.zeros((2 * ny * 16, cols), F32)
     second = jnp.zeros((2 * ny * 16, cols), F32)
     for g in range(key_heads):
-        rows = g_in[:, g * 16 : (g + 1) * 16, :].reshape(2 * ny * 16, LANES)
+        rows = g_all[:, g * 16 : (g + 1) * 16, :].reshape(2 * ny * 16, LANES)
         first += mm(rows, w_out[:, 2 * g * LANES : (2 * g + 1) * LANES], NT)
         second += mm(rows, w_out[:, (2 * g + 1) * LANES : (2 * g + 2) * LANES], NT)
     part = first.reshape(2 * ny, 2, PAD, cols)[:, 0] + second.reshape(2 * ny, 2, PAD, cols)[:, 1]
@@ -316,80 +332,50 @@
             send(p_src.at[c, x], p_in.at[my_c * nx + my_x], 4, place_of(x, my_y, my_z, c))
     send(p_src.at[other, my_x], p_in.at[my_c * nx + my_x], 4, sibling)
     p_in[my_c * nx + my_x] = p_src[my_c, my_x]
-    span = pl.ds(pl.multiple_of(xs[1] * x_width, x_width), x_width)
-    send(down_hbm.at[:, :, span], w_down.at[my_x], 15, place_of(xs[1], my_y, my_z, my_c))
-
     whole_wait(r0_in.at[pl.ds(0, ny - 1)], recv_sem.at[0])
-    low = iota((PAD, LANES), 1) < LANES // 2
-    ids = jnp.zeros((PAD, LANES), F32)
-    picks_w = jnp.zeros((PAD, LANES), F32)
-    for y in range(ny):
-        both = r0_in[y]
-        ids = ids + pltpu.roll(jnp.where(low, both, 0.0), y * top, 1)
-        picks_w = picks_w + pltpu.roll(
-            jnp.where(low, 0.0, both), (y * top + LANES // 2) % LANES, 1
-        )
+    ids = jnp.sum(r0_in[...], axis=0)
     r1_src[...] = ids
     for zc in zcs:
         send(r1_src, r1_in.at[my_zc], 3, at_zc(zc))
     r1_in[my_zc] = ids
 
-    def owner_of(t):
-        return jnp.floor((t - 1.0) * 0.5).astype(jnp.int32) - my_y * nzc
-
+    here = y_chunks * ROWS
     sel_row = iota((32, LANES), 0)
     pick = jnp.bitwise_and(sel_row, 15)
     source = SRC * my_x + jnp.right_shift(sel_row, 4)
     sel = ((iota((32, LANES), 1) == source * top + pick) & (pick < top)).astype(F32)
-    spread = (iota((PAD, flat), 0) == jnp.bitwise_and(iota((PAD, flat), 1), 7)).astype(F32)
-    flat_src = jnp.bitwise_and(jnp.right_shift(iota((16, flat), 1), 3), 1)
+    spread = (iota((PAD, here), 0) == jnp.bitwise_and(iota((PAD, here), 1), 7)).astype(F32)
+    of_source = jnp.bitwise_and(jnp.right_shift(iota((16, here), 1), 3), 1)
     wide = mm(mm(sel, ids, NT, EXACT), spread, precision=EXACT)
-    owner = owner_of(jnp.where(flat_src == 0, wide[0:16], wide[16:32]))
-    zc_row = iota((nzc, flat), 0)
-    hit = jnp.zeros((nzc, flat), F32)
+    owner = jnp.where(of_source == 0, wide[0:16], wide[16:32])
+    owner = jnp.floor((owner - 1.0) * 0.5).astype(jnp.int32)
+    owner_row = iota((owners, here), 0)
+    hit = jnp.zeros((owners, here), F32)
     for j in range(top):
-        hit = hit + jnp.where(zc_row == owner[j : j + 1, :], 1.0, 0.0)
-    msg_row = iota((msg, flat), 0)
-    msg_col = iota((msg, flat), 1)
-    match = (jnp.bitwise_and(msg_row, chunks - 1) == jnp.right_shift(msg_col, 4)) & (
-        msg_row // chunks == jnp.bitwise_and(jnp.right_shift(msg_col, 3), 1)
+        hit = hit + jnp.where(owner_row == owner[j : j + 1, :], 1.0, 0.0)
+    each = (iota((owners * 4, owners), 1) == jnp.right_shift(iota((owners * 4, owners), 0), 2))
+    row = iota((owners * 4, here), 0)
+    col = iota((owners * 4, here), 1)
+    match = (jnp.bitwise_and(jnp.right_shift(row, 1), 1) == jnp.bitwise_and(jnp.right_shift(col, 3), 1)) & (
+        jnp.bitwise_and(row, 1) == jnp.right_shift(col, 4)
     )
-    match = match.astype(F32)
-    for zc in range(nzc):
-        place[zc * msg : (zc + 1) * msg, :] = (hit[zc : zc + 1, :] * match).astype(BF16)
-
-    mixed_rows = ny * x_chunks * PAD
-    sel_row = iota((ny * 16, LANES), 0)
-    pick = jnp.bitwise_and(sel_row, 15)
-    source = jnp.right_shift(sel_row, 4)
-    sel = ((iota((ny * 16, LANES), 1) == source * top + pick) & (pick < top)).astype(F32)
-    spread = (
-        iota((PAD, mixed_rows), 0) == jnp.bitwise_and(iota((PAD, mixed_rows), 1), 7)
-    ).astype(F32)
-    of_source = iota((16, mixed_rows), 1) // (x_chunks * PAD)
-
-    def table(t):
-        wide = mm(mm(sel, t, NT, EXACT), spread, precision=EXACT)
-        kept = jnp.zeros((16, mixed_rows), F32)
-        for y in range(ny):
-            kept = jnp.where(of_source == y, wide[y * 16 : (y + 1) * 16], kept)
-        return kept
-
-    owner = owner_of(table(ids))
-    weight = table(picks_w)
-    zc_row = iota((nzc, mixed_rows), 0)
-    hit_w = jnp.zeros((nzc, mixed_rows), F32)
+    place[...] = jnp.where(match, mm(each.astype(BF16), hit.astype(BF16)), 0.0).astype(BF16)
+
+    own_ids = small[0]
+    own_weight = small[1]
+    lane = iota((PAD, LANES), 1)
+    share = jnp.zeros((PAD, owners), F32)
     for j in range(top):
-        hit_w = hit_w + jnp.where(zc_row == owner[j : j + 1, :], weight[j : j + 1, :], 0.0)
-    weigh_t = hit_w.T
-    hi = weigh_t.astype(BF16)
-    lo = (weigh_t - hi.astype(F32)).astype(BF16)
-    open_up = (iota((nzc, back), 0) == iota((nzc, back), 1) // msg).astype(BF16)
-    w_row = iota((mixed_rows, back), 0)
-    w_col = iota((mixed_rows, back), 1)
-    kept = jnp.right_shift(w_row, 3) == jnp.bitwise_and(w_col, msg - 1)
-    weigh[0] = jnp.where(kept, mm(hi, open_up), 0.0).astype(BF16)
-    weigh[1] = jnp.where(kept, mm(lo, open_up), 0.0).astype(BF16)
+        named = jnp.floor((own_ids[:, j : j + 1] - 1.0) * 0.5).astype(jnp.int32)
+        share = share + jnp.where(lane == named, own_weight[:, j : j + 1], 0.0)
+    hi = share.astype(BF16).astype(F32)
+    open_up = iota((owners, back), 0) == jnp.right_shift(iota((owners, back), 1), 2)
+    both = mm(jnp.concatenate([hi, share - hi], axis=0).astype(BF16), open_up.astype(BF16))
+    row = iota((x_chunks * PAD, back), 0)
+    kept = jnp.right_shift(row, 3) == jnp.bitwise_and(iota((x_chunks * PAD, back), 1), 3)
+    for n in range(2):
+        tall = jnp.concatenate([both[n * PAD : (n + 1) * PAD]] * x_chunks, axis=0)
+        weigh[n] = jnp.where(kept, tall, 0.0).astype(BF16)
 
     mix_row = iota((2 * cols, 2 * cols), 0)
     mix_col = iota((2 * cols, 2 * cols), 1)
@@ -413,16 +399,55 @@
         attn.append(total.astype(BF16))
     attn = mm(jnp.concatenate(attn, axis=1), mix)
     base_rows = [b_in[SRC * my_x + s].astype(F32) for s in range(SRC)]
+    parts = []
     for i in range(y_chunks):
         base = jnp.concatenate([rows[i * PAD : (i + 1) * PAD] for rows in base_rows], axis=0)
-        c_src[i] = (base + attn[:, i * LANES : (i + 1) * LANES]).astype(BF16)
-    for y in ys:
-        send(c_src, c_in.at[my_y], 5, place_of(my_x, y, my_z, my_c))
-    c_in[my_y] = c_src[...]
+        parts.append(base + attn[:, i * LANES : (i + 1) * LANES])
+    carried = jnp.concatenate(parts, axis=0).astype(BF16)
+
+    m3_src[...] = mm(place[...], carried).astype(BF16).reshape(owners, 4, LANES)
+    for i, z in enumerate(z_to):
+        for c in (my_c, other):
+            for dy in Y_ORDER:
+                y = lax.rem(my_y + dy, ny)
+                to = place_of(my_x, y, z, c)
+                src = m3_src.at[to[0]]
+                dst = m3_in.at[i * 2 + my_c, my_y]
+                if order[i] or dy or c is other:
+                    send(src, dst, 6 + i // 4, to)
+                else:
+                    pltpu.make_async_copy(src, dst, recv_sem.at[6 + i // 4]).start()
+
+    half = my_y - SRC * my_x
+    wide = carried.astype(F32)
+    to_x = my_y // SRC
+    k_dst = k_in.at[my_y - SRC * to_x]
+    k_copies = []
+    for n in range(SRC):
+        rows = [wide[i * ROWS + n * PAD : i * ROWS + (n + 1) * PAD] for i in range(y_chunks)]
+        k_src[n] = jnp.concatenate(rows, axis=0).astype(BF16)
+        away = remote(k_src.at[n], k_dst, 14, place_of(to_x, SRC * my_x + n, my_z, my_c))
+        keep = pltpu.make_async_copy(k_src.at[n], k_dst, recv_sem.at[14])
+        k_copies.append(away)
+
+        @pl.when(half == n)
+        def _():
+            keep.start()
+
+        @pl.when(half != n)
+        def _():
+            away.start()
+
+    span = pl.ds(pl.multiple_of(xs[1] * x_width, x_width), x_width)
+    send(down_hbm.at[:, :, span], w_down.at[my_x], 15, place_of(xs[1], my_y, my_z, my_c))
 
     whole_wait(r1_in.at[pl.ds(0, nzc - 1)], recv_sem.at[3])
     slot = iota((groups * block, nzc), 0)
-    slot_zc = (slot // block) * 8 + jnp.bitwise_and(jnp.right_shift(slot, 1), 7)
+    slot_i = (slot // block) * 4 + jnp.bitwise_and(jnp.right_shift(slot, 2), 3)
+    slot_z = jnp.zeros_like(slot)
+    for i, z in enumerate(z_from):
+        slot_z = jnp.where(slot_i == i, z, slot_z)
+    slot_zc = slot_z * 2 + jnp.bitwise_and(jnp.right_shift(slot, 1), 1)
     of_zc = (slot_zc == iota((groups * block, nzc), 1)).astype(BF16)
     slot = iota((groups * block, LANES), 0)
     slot_x = jnp.right_shift(jnp.bitwise_and(slot, block - 1), 4)
@@ -438,53 +463,29 @@
             jnp.sum(found, axis=1, keepdims=True), (groups * block, LANES)
         )
 
-    whole_wait(c_in.at[pl.ds(0, ny - 1)], recv_sem.at[5])
-    squares = jnp.zeros((ROWS, LANES), F32)
-    for ch in range(chunks):
-        c = c_in[ch // y_chunks, ch % y_chunks].astype(F32)
-        squares = squares + c * c
-    norm = lax.rsqrt(jnp.sum(squares, axis=1, keepdims=True) / width + 1e-06)
-    for ch in range(chunks):
-        c = c_in[ch // y_chunks, ch % y_chunks].astype(F32)
-        n_scr[ch * 16 : (ch + 1) * 16, :] = (
-            c * norm * ffn_gain[:, ch * LANES : (ch + 1) * LANES]
-        ).astype(BF16)
-
-    m3_src[...] = mm(place[...], n_scr[...]).astype(BF16).reshape(nzc, msg, LANES)
-    my_group = my_zc // 8
-    for zc in zcs:
-        send(m3_src.at[zc], m3_in.at[my_zc], 6 + my_group, at_zc(zc))
-    m3_own = pltpu.make_async_copy(m3_src.at[my_zc], m3_in.at[my_zc], recv_sem.at[6 + my_group])
-    m3_own.start()
-
-    half = my_y - SRC * my_x
-    home = (half >= 0) & (half < SRC)
-    for x in range(nx):
-        tiles = []
-        for ch in range(x * x_chunks, (x + 1) * x_chunks):
-            c = c_in[ch // y_chunks, ch % y_chunks].astype(F32)
-            tiles.append(jnp.where(half == 0, c[0:PAD], c[PAD : 2 * PAD]))
-        k_src[x] = jnp.concatenate(tiles, axis=0).astype(BF16)
-    k_away = [remote(k_src.at[x], k_in, 14, place_of(x, my_y, my_z, my_c)) for x in xs]
-    k_own = pltpu.make_async_copy(k_src.at[my_x], k_in, recv_sem.at[14])
-
-    @pl.when(home)
-    def _():
-        k_own.start()
-        for copy in k_away:
-            copy.start()
-
     turn_row = iota((flat, flat), 0)
     turn_col = iota((flat, flat), 1)
-    unflat = (jnp.bitwise_and(turn_row, 15) == turn_col // chunks) & (
-        jnp.right_shift(turn_row, 4) == jnp.bitwise_and(turn_col, chunks - 1)
+    turn_ch = jnp.right_shift(turn_row, 4)
+    turn_slot = jnp.bitwise_and(turn_row, 15)
+    unflat = turn_col == (
+        (turn_slot // 2) * (ny * 4)
+        + (turn_ch // y_chunks) * 4
+        + jnp.bitwise_and(turn_slot, 1) * y_chunks
+        + turn_ch % y_chunks
     )
     unflat = unflat.astype(BF16)
     for n in range(groups):
         whole_wait(m3_in.at[pl.ds(n * 8, 8)], recv_sem.at[6 + n])
-        turned = mm(unflat, m3_in[n * 8 : (n + 1) * 8].reshape(flat, LANES)).astype(BF16)
+        turned = mm(unflat, m3_in[n * 8 : (n + 1) * 8].reshape(flat, LANES))
+        squares = jnp.zeros((16, LANES), F32)
         for ch in range(chunks):
-            x_src[n, :, ch * LANES : (ch + 1) * LANES] = turned[ch * 16 : (ch + 1) * 16]
+            c = turned[ch * 16 : (ch + 1) * 16]
+            squares = squares + c * c
+        norm = lax.rsqrt(jnp.sum(squares, axis=1, keepdims=True) / width + 1e-06)
+        for ch in range(chunks):
+            c = turned[ch * 16 : (ch + 1) * 16]
+            span = slice(ch * LANES, (ch + 1) * LANES)
+            x_src[n, :, span] = (c * norm * ffn_gain[:, span]).astype(BF16)
         for x in near_first:
             send(x_src.at[n], x_in.at[n, my_x], 8 + n, place_of(x, my_y, my_z, my_c))
         x_in[n, my_x] = x_src[n]
@@ -530,45 +531,32 @@
             for ch in range(x_chunks)
         ]
         turned = mm(flatten, jnp.concatenate(tiles, axis=0)).astype(BF16)
-        m6_src[n * 8 : (n + 1) * 8] = turned.reshape(8, msg, LANES)
-        for i in range(8):
-            zc = n * 8 + i
-            away = remote(m6_src.at[zc], m6_in.at[my_zc], 12, at_zc(zc))
-            keep = pltpu.make_async_copy(m6_src.at[zc], m6_in.at[my_zc], recv_sem.at[12])
-
-            @pl.when(zc == my_zc)
-            def _():
-                keep.start()
-
-            @pl.when(zc != my_zc)
-            def _():
-                away.start()
-
-    whole_wait(m6_in, recv_sem.at[12])
+        m6_src[n * 8 : (n + 1) * 8] = turned.reshape(8, ny, 4, LANES)
+        for i in range(n * 4, (n + 1) * 4):
+            for c in (my_c, other):
+                for dy in Y_ORDER:
+                    y = lax.rem(my_y + dy, ny)
+                    src = m6_src.at[i * 2 + c, y]
+                    if order[i] or dy or c is other:
+                        send(src, m6_in.at[ep], 12, place_of(my_x, y, z_from[i], c))
+                    else:
+                        m6_in[ep] = m6_src[i * 2 + my_c, my_y]
+
+    whole_wait(k_in, recv_sem.at[14])
+    whole_wait(m6_in.at[pl.ds(0, owners - 1)], recv_sem.at[12])
     rows = m6_in[...].reshape(back, LANES)
-    mixed = (mm(weigh[0], rows) + mm(weigh[1], rows)).reshape(ny, x_chunks * PAD, LANES)
-    m7_own[...] = mixed
-    m7_src[...] = mixed.astype(BF16)
-    for y in ys:
-        send(m7_src.at[y], m7_in.at[my_y], 13, place_of(my_x, y, my_z, my_c))
+    mixed = mm(weigh[0], rows) + mm(weigh[1], rows)
+    mixed = mixed + k_in[...].reshape(x_chunks * PAD, LANES).astype(F32)
+    for i in range(x_chunks):
+        out[:, i * LANES : (i + 1) * LANES] = mixed[i * PAD : i * PAD + count].astype(BF16)
 
     for copy in sent:
         copy.wait_send()
-    whole_wait(m6_src.at[pl.ds(0, nzc - 1)], send_sem.at[12])
-
-    @pl.when(home)
-    def _():
-        for copy in k_away:
+    for n, copy in enumerate(k_copies):
+
+        @pl.when(half != n)
+        def _():
             copy.wait_send()
-
-    whole_wait(k_in, recv_sem.at[14])
-    whole_wait(m7_in.at[pl.ds(0, ny - 1)], recv_sem.at[13])
-    total = m7_own[my_y]
-    for y in ys:
-        total = total + m7_in[y].astype(F32)
-    total = (total + k_in[...].astype(F32)).reshape(x_chunks, PAD, LANES)
-    for i in range(x_chunks):
-        out[:, i * LANES : (i + 1) * LANES] = total[i, 0:count].astype(BF16)
 
 
 def shards(
@@ -603,8 +591,7 @@
     chunks = width // LANES
     y_chunks = chunks // ny
     x_chunks = chunks // nx
-    msg = SRC * chunks
-    flat = 16 * chunks
+    owners = ny * nzc
     cols = nzc // 2 * 16
     groups = nzc // 8
     block = nx * 16
@@ -644,28 +631,24 @@
         pltpu.VMEM((PAD, LANES), F32),
         pltpu.VMEM((nzc, PAD, LANES), F32),
         pltpu.VMEM((heads * PAD, LANES), BF16),
+        pltpu.VMEM((heads * count, LANES), BF16),
+        pltpu.VMEM((2 * ny, heads * count, LANES), BF16),
         pltpu.VMEM((2 * ny, heads * PAD, LANES), BF16),
         pltpu.VMEM((2, nx, ROWS, cols), F32),
         pltpu.VMEM((2 * nx, ROWS, cols), F32),
-        pltpu.VMEM((y_chunks, ROWS, LANES), BF16),
-        pltpu.VMEM((ny, y_chunks, ROWS, LANES), BF16),
-        pltpu.VMEM((nx, x_chunks * PAD, LANES), BF16),
-        pltpu.VMEM((x_chunks * PAD, LANES), BF16),
-        pltpu.VMEM((flat, LANES), BF16),
-        pltpu.VMEM((nzc * msg, flat), BF16),
-        pltpu.VMEM((2, ny * x_chunks * PAD, nzc * msg), BF16),
+        pltpu.VMEM((SRC, y_chunks * PAD, LANES), BF16),
+        pltpu.VMEM((SRC, y_chunks * PAD, LANES), BF16),
+        pltpu.VMEM((owners * 4, y_chunks * ROWS), BF16),
+        pltpu.VMEM((2, x_chunks * PAD, owners * 4), BF16),
         pltpu.VMEM((2, groups * block, LANES), F32),
-        pltpu.VMEM((nzc, msg, LANES), BF16),
-        pltpu.VMEM((nzc, msg, LANES), BF16),
+        pltpu.VMEM((owners, 4, LANES), BF16),
+        pltpu.VMEM((nzc, ny, 4, LANES), BF16),
         pltpu.VMEM((groups, 16, width), BF16),
         pltpu.VMEM((groups, nx, 16, width), BF16),
         pltpu.VMEM((groups, block, LANES), BF16),
         pltpu.VMEM((groups, nx, block, LANES), BF16),
-        pltpu.VMEM((nzc, msg, LANES), BF16),
-        pltpu.VMEM((nzc, msg, LANES), BF16),
-        pltpu.VMEM((ny, x_chunks * PAD, LANES), F32),
-        pltpu.VMEM((ny, x_chunks * PAD, LANES), BF16),
-        pltpu.VMEM((ny, x_chunks * PAD, LANES), BF16),
+        pltpu.VMEM((nzc, ny, 4, LANES), BF16),
+        pltpu.VMEM((owners, 4, LANES), BF16),
         pltpu.SemaphoreType.DMA((len(small_operands),)),
         pltpu.SemaphoreType.DMA((8,)),
         pltpu.SemaphoreType.DMA((17,)),

time: 62.9 us -> 59.3 us (0.943)
  Pallas kernels: 61.5 us -> 57.8 us
    pallas_call x1, Pallas kernels: 61.5 us -> 57.8 us  [shards(): pl.pallas_call(functools.partial(kernel, nx, ny, nzc, top), out_shape=jax...]
where the time goes in v3:
time: 59.3 us; the launch traced here: 59.1 us
  Pallas kernels  57.8 us (97%)
  local copies, waits for them, and re-layouts  1.3 us (2%)
    pallas_call x1, Pallas kernels, shards(): pl.pallas_call(functools.partial(kernel, nx, ny, nzc, top), out_shape=jax...  57.8 us
    unnamed x1, local copies, waits for them, and re-layouts  1.3 us

profile of v3, /device:TPU:1, one launch (start us, length us, event | category | flops | bytes accessed | tf_op | source)
XLA Modules:
  0.0 59.1 jit_solution(7530308596350773839)
XLA Ops:
  0.0 57.8 %decode_layer.1 = bf16[6,512]{1,0:T(8,128)(2,1)} custom-call(bf16[6,2048]{1,0:T(8,128)(2,1)} %residual_hbm.1, bf16[6,512]{1,0:T(8,128)(2,1)} %query_hbm.1, bf16[6,512]{1,0:T(8,128)(2,1)} %keys_hbm.1, bf16[6,1024]{1,0:T(8,128)(2,1)} %values_hbm.1, bf16[6,1024]{1,0:T(8,128)(2,1)} %out_gate_hbm.1, f32[6,8]{1,0:T(8,128)} %beta_logit_hbm.1, ...), custom_call_target="tpu_custom_call" | custom-call | tf_op jit(solution)/shard_map/decode_layer/pallas_call | solution.py:657
  57.8 1.3 %copy.22 = bf16[6,512]{1,0:T(8,128)(2,1)} copy(bf16[6,512]{1,0:T(8,128)(2,1)} %decode_layer.1) | data formatting | bytes 12288

commit v4 on v3

--- a/solution.py
+++ b/solution.py
@@ -15,6 +15,8 @@
 PAD = 8
 SRC = 2
 Z_ORDER = (0, 1, 7, 2, 6, 3, 5, 4)
+GROUP_Z = 2
+GROUP_ORDER = (0, 1, 2, 3)
 Y_ORDER = (4, 3, 5, 2, 6, 1, 7, 0)
 ROWS = SRC * PAD
 NT = (((1,), (1,)), ((), ()))
@@ -122,12 +124,13 @@
     heads = 2 * key_heads
     nz = nzc // 2
     cols = nz * 16
-    msg = SRC * chunks
-    flat = 16 * chunks
+    per_x = GROUP_Z * 2 * SRC
+    flat = per_x * chunks
     owners = ny * nzc
     back = owners * 4
-    groups = nzc // 8
-    block = nx * 16
+    groups = nz // GROUP_Z
+    g_zc = 2 * GROUP_Z
+    block = nx * per_x
 
     ep = lax.axis_index("ep")
     my_x = lax.axis_index("tp")
@@ -202,10 +205,12 @@
     w_own.start()
 
     barrier = pltpu.get_barrier_semaphore()
-    peers = [at_zc(zc) for zc in zcs]
-    for c in (my_c, other):
-        peers += [place_of(my_x, y, my_z, c) for y in ys]
-        peers += [place_of(x, my_y, my_z, c) for x in xs]
+    peers = [
+        place_of(my_x, lax.rem(my_y + d, ny), my_z, c) for d in Y_ORDER for c in (my_c, other) if d
+    ]
+    peers += [place_of(my_x, my_y, lax.rem(my_z + d, nz), my_c) for d in Y_ORDER if d]
+    peers += [place_of(x, my_y, my_z, my_c) for x in xs]
+    peers.append(sibling)
     for peer in peers:
         pl.semaphore_signal(barrier, inc=1, device_id=peer, device_id_type=MESH)
     pl.semaphore_wait(barrier, len(peers))
@@ -217,6 +222,9 @@
     for x in near_first[0:2]:
         span = pl.ds(pl.multiple_of(x * x_width, x_width), x_width)
         send(down_hbm.at[:, :, span], w_down.at[my_x], 15, place_of(x, my_y, my_z, my_c))
+    far = place_of(xs[1], my_y, my_z, my_c)
+    far_span = pl.ds(pl.multiple_of(xs[1] * x_width, x_width), x_width)
+    send(down_hbm.at[0, :, far_span], w_down.at[my_x, 0], 15, far)
 
     stage[...] = jnp.zeros_like(stage)
     small[...] = jnp.zeros_like(small)
@@ -281,7 +289,7 @@
 
     small[0, 0:count, 0:top] = (route_ids[...] + 1).astype(F32)
     small[1, 0:count, 0:top] = route_weight[...]
-    r0_src[...] = pltpu.roll(small[0], my_y * top, 1)
+    r0_src[...] = pltpu.roll(small[0], my_y * top, 1).astype(BF16)
     stage[0:count, r_at * LANES : r_at * LANES + width] = residual[...].astype(F32)
     for y in range(ny):
         at = (r_at + y * y_chunks) * LANES
@@ -333,11 +341,11 @@
     send(p_src.at[other, my_x], p_in.at[my_c * nx + my_x], 4, sibling)
     p_in[my_c * nx + my_x] = p_src[my_c, my_x]
     whole_wait(r0_in.at[pl.ds(0, ny - 1)], recv_sem.at[0])
-    ids = jnp.sum(r0_in[...], axis=0)
-    r1_src[...] = ids
+    ids = jnp.sum(r0_in[...].astype(F32), axis=0)
+    r1_src[...] = ids.astype(BF16)
     for zc in zcs:
         send(r1_src, r1_in.at[my_zc], 3, at_zc(zc))
-    r1_in[my_zc] = ids
+    r1_in[my_zc] = r1_src[...]
 
     here = y_chunks * ROWS
     sel_row = iota((32, LANES), 0)
@@ -414,9 +422,9 @@
                 src = m3_src.at[to[0]]
                 dst = m3_in.at[i * 2 + my_c, my_y]
                 if order[i] or dy or c is other:
-                    send(src, dst, 6 + i // 4, to)
+                    send(src, dst, 20 + i // GROUP_Z, to)
                 else:
-                    pltpu.make_async_copy(src, dst, recv_sem.at[6 + i // 4]).start()
+                    pltpu.make_async_copy(src, dst, recv_sem.at[20 + i // GROUP_Z]).start()
 
     half = my_y - SRC * my_x
     wide = carried.astype(F32)
@@ -438,23 +446,24 @@
         def _():
             away.start()
 
-    span = pl.ds(pl.multiple_of(xs[1] * x_width, x_width), x_width)
-    send(down_hbm.at[:, :, span], w_down.at[my_x], 15, place_of(xs[1], my_y, my_z, my_c))
+    send(down_hbm.at[1, :, far_span], w_down.at[my_x, 1], 15, far)
 
     whole_wait(r1_in.at[pl.ds(0, nzc - 1)], recv_sem.at[3])
     slot = iota((groups * block, nzc), 0)
-    slot_i = (slot // block) * 4 + jnp.bitwise_and(jnp.right_shift(slot, 2), 3)
+    slot_i = (slot // block) * GROUP_Z + jnp.bitwise_and(
+        jnp.right_shift(slot, 2), GROUP_Z - 1
+    )
     slot_z = jnp.zeros_like(slot)
     for i, z in enumerate(z_from):
         slot_z = jnp.where(slot_i == i, z, slot_z)
     slot_zc = slot_z * 2 + jnp.bitwise_and(jnp.right_shift(slot, 1), 1)
     of_zc = (slot_zc == iota((groups * block, nzc), 1)).astype(BF16)
     slot = iota((groups * block, LANES), 0)
-    slot_x = jnp.right_shift(jnp.bitwise_and(slot, block - 1), 4)
+    slot_x = jnp.bitwise_and(slot, block - 1) // per_x
     slot_y = SRC * slot_x + jnp.bitwise_and(slot, 1)
     lane = iota((groups * block, LANES), 1)
     of_y = (lane >= slot_y * top) & (lane < slot_y * top + top)
-    arrived = r1_in[...]
+    arrived = r1_in[...].astype(F32)
     for e in range(2):
         named = (2 * ep + 1 + e).astype(F32)
         found = jnp.sum(jnp.where(arrived == named, 1.0, 0.0), axis=1).astype(BF16)
@@ -465,8 +474,8 @@
 
     turn_row = iota((flat, flat), 0)
     turn_col = iota((flat, flat), 1)
-    turn_ch = jnp.right_shift(turn_row, 4)
-    turn_slot = jnp.bitwise_and(turn_row, 15)
+    turn_ch = turn_row // per_x
+    turn_slot = turn_row % per_x
     unflat = turn_col == (
         (turn_slot // 2) * (ny * 4)
         + (turn_ch // y_chunks) * 4
@@ -474,26 +483,38 @@
         + turn_ch % y_chunks
     )
     unflat = unflat.astype(BF16)
-    for n in range(groups):
-        whole_wait(m3_in.at[pl.ds(n * 8, 8)], recv_sem.at[6 + n])
-        turned = mm(unflat, m3_in[n * 8 : (n + 1) * 8].reshape(flat, LANES))
-        squares = jnp.zeros((16, LANES), F32)
+    for n in GROUP_ORDER:
+        whole_wait(m3_in.at[pl.ds(n * g_zc, g_zc)], recv_sem.at[20 + n])
+        turned = mm(unflat, m3_in[n * g_zc : (n + 1) * g_zc].reshape(flat, LANES))
+        squares = jnp.zeros((per_x, LANES), F32)
         for ch in range(chunks):
-            c = turned[ch * 16 : (ch + 1) * 16]
+            c = turned[ch * per_x : (ch + 1) * per_x]
             squares = squares + c * c
         norm = lax.rsqrt(jnp.sum(squares, axis=1, keepdims=True) / width + 1e-06)
         for ch in range(chunks):
-            c = turned[ch * 16 : (ch + 1) * 16]
+            c = turned[ch * per_x : (ch + 1) * per_x]
             span = slice(ch * LANES, (ch + 1) * LANES)
             x_src[n, :, span] = (c * norm * ffn_gain[:, span]).astype(BF16)
         for x in near_first:
-            send(x_src.at[n], x_in.at[n, my_x], 8 + n, place_of(x, my_y, my_z, my_c))
+            send(x_src.at[n], x_in.at[n, my_x], 24 + n, place_of(x, my_y, my_z, my_c))
         x_in[n, my_x] = x_src[n]
 
+    back_row = iota((block * x_chunks, block * x_chunks), 0)
+    back_col = iota((block * x_chunks, block * x_chunks), 1)
+    each_zc = ny * x_chunks
+    row_y = (back_row % each_zc) // x_chunks
+    slot = back_col % per_x
+    flatten = (
+        (back_row // each_zc == jnp.right_shift(slot, 1))
+        & (row_y == SRC * (back_col // (per_x * x_chunks)) + jnp.bitwise_and(slot, 1))
+        & (back_row % x_chunks == (back_col // per_x) % x_chunks)
+    )
+    flatten = flatten.astype(BF16)
     for load in w_loads:
         load.wait()
-    for n in range(groups):
-        whole_wait(x_in.at[n, pl.ds(0, nx - 1)], recv_sem.at[8 + n])
+
+    def hidden_of(n):
+        whole_wait(x_in.at[n, pl.ds(0, nx - 1)], recv_sem.at[24 + n])
         both = mm(x_in[n].reshape(block, width), w_in[...])
         hidden = jnp.zeros((block, LANES), F32)
         for e in range(2):
@@ -501,38 +522,29 @@
             up = both[:, (2 + e) * LANES : (3 + e) * LANES]
             hidden = hidden + silu(gate) * up * masks[e, n * block : (n + 1) * block]
         h_src[n] = hidden.astype(BF16)
-        for x in xs:
-            send(h_src.at[n], h_in.at[n, my_x], 10 + n, place_of(x, my_y, my_z, my_c))
+        for x in near_first:
+            send(h_src.at[n], h_in.at[n, my_x], 28 + n, place_of(x, my_y, my_z, my_c))
         h_in[n, my_x] = h_src[n]
 
-    back_row = iota((block * x_chunks, block * x_chunks), 0)
-    back_col = iota((block * x_chunks, block * x_chunks), 1)
-    row_y = (back_row % msg) // x_chunks
-    slot = jnp.bitwise_and(back_col, 15)
-    flatten = (
-        (back_row // msg == jnp.right_shift(slot, 1))
-        & (row_y == SRC * (back_col // (16 * x_chunks)) + jnp.bitwise_and(slot, 1))
-        & (back_row % x_chunks == jnp.right_shift(back_col, 4) % x_chunks)
-    )
-    flatten = flatten.astype(BF16)
-    whole_wait(w_down.at[pl.ds(0, nx - 1)], recv_sem.at[15])
-    for n in range(groups):
-        whole_wait(h_in.at[n, pl.ds(0, nx - 1)], recv_sem.at[10 + n])
-        total = jnp.zeros((block, x_width), F32)
+    def output_of(n):
+        whole_wait(h_in.at[n, pl.ds(0, nx - 1)], recv_sem.at[28 + n])
+        parts = []
         for x in range(nx):
             h = h_in[n, x].astype(F32)
             for e in range(2):
-                chosen = (h * masks[e, n * block : (n + 1) * block]).astype(BF16)
-                total = total + mm(chosen, w_down[x, e])
-        total = total.astype(BF16)
+                parts.append(h * masks[e, n * block : (n + 1) * block])
+        total = mm(
+            jnp.concatenate(parts, axis=1).astype(BF16),
+            w_down[...].reshape(nx * 2 * LANES, x_width),
+        )
         tiles = [
-            total[x * 16 : (x + 1) * 16, ch * LANES : (ch + 1) * LANES]
+            total[x * per_x : (x + 1) * per_x, ch * LANES : (ch + 1) * LANES]
             for x in range(nx)
             for ch in range(x_chunks)
         ]
-        turned = mm(flatten, jnp.concatenate(tiles, axis=0)).astype(BF16)
-        m6_src[n * 8 : (n + 1) * 8] = turned.reshape(8, ny, 4, LANES)
-        for i in range(n * 4, (n + 1) * 4):
+        turned = mm(flatten, jnp.concatenate(tiles, axis=0).astype(BF16)).astype(BF16)
+        m6_src[n * g_zc : (n + 1) * g_zc] = turned.reshape(g_zc, ny, 4, LANES)
+        for i in range(n * GROUP_Z, (n + 1) * GROUP_Z):
             for c in (my_c, other):
                 for dy in Y_ORDER:
                     y = lax.rem(my_y + dy, ny)
@@ -541,6 +553,16 @@
                         send(src, m6_in.at[ep], 12, place_of(my_x, y, z_from[i], c))
                     else:
                         m6_in[ep] = m6_src[i * 2 + my_c, my_y]
+
+    lag = groups
+    for k, n in enumerate(GROUP_ORDER):
+        hidden_of(n)
+        if k == lag - 1:
+            whole_wait(w_down.at[pl.ds(0, nx - 1)], recv_sem.at[15])
+        if k >= lag:
+            output_of(GROUP_ORDER[k - lag])
+    for n in GROUP_ORDER[groups - lag :]:
+        output_of(n)
 
     whole_wait(k_in, recv_sem.at[14])
     whole_wait(m6_in.at[pl.ds(0, owners - 1)], recv_sem.at[12])
@@ -593,8 +615,9 @@
     x_chunks = chunks // nx
     owners = ny * nzc
     cols = nzc // 2 * 16
-    groups = nzc // 8
-    block = nx * 16
+    groups = nzc // 2 // GROUP_Z
+    per_x = GROUP_Z * 2 * SRC
+    block = nx * per_x
     stage_tiles = 2 * key_heads + 2 * heads + chunks
     vmem = pl.BlockSpec(memory_space=pltpu.VMEM)
     hbm = pl.BlockSpec(memory_space=pltpu.HBM)
@@ -624,12 +647,12 @@
         pltpu.VMEM((width, 4 * LANES), BF16),
         pltpu.VMEM((nx, 2, LANES, width // nx), BF16),
         pltpu.VMEM((cols, heads * LANES), BF16),
-        pltpu.VMEM((PAD, LANES), F32),
-        pltpu.VMEM((ny, PAD, LANES), F32),
+        pltpu.VMEM((PAD, LANES), BF16),
+        pltpu.VMEM((ny, PAD, LANES), BF16),
         pltpu.VMEM((ny, y_chunks * PAD, LANES), BF16),
         pltpu.VMEM((ny, y_chunks * PAD, LANES), BF16),
-        pltpu.VMEM((PAD, LANES), F32),
-        pltpu.VMEM((nzc, PAD, LANES), F32),
+        pltpu.VMEM((PAD, LANES), BF16),
+        pltpu.VMEM((nzc, PAD, LANES), BF16),
         pltpu.VMEM((heads * PAD, LANES), BF16),
         pltpu.VMEM((heads * count, LANES), BF16),
         pltpu.VMEM((2 * ny, heads * count, LANES), BF16),
@@ -643,20 +666,20 @@
         pltpu.VMEM((2, groups * block, LANES), F32),
         pltpu.VMEM((owners, 4, LANES), BF16),
         pltpu.VMEM((nzc, ny, 4, LANES), BF16),
-        pltpu.VMEM((groups, 16, width), BF16),
-        pltpu.VMEM((groups, nx, 16, width), BF16),
+        pltpu.VMEM((groups, per_x, width), BF16),
+        pltpu.VMEM((groups, nx, per_x, width), BF16),
         pltpu.VMEM((groups, block, LANES), BF16),
         pltpu.VMEM((groups, nx, block, LANES), BF16),
         pltpu.VMEM((nzc, ny, 4, LANES), BF16),
         pltpu.VMEM((owners, 4, LANES), BF16),
         pltpu.SemaphoreType.DMA((len(small_operands),)),
         pltpu.SemaphoreType.DMA((8,)),
-        pltpu.SemaphoreType.DMA((17,)),
-        pltpu.SemaphoreType.DMA((17,)),
+        pltpu.SemaphoreType.DMA((32,)),
+        pltpu.SemaphoreType.DMA((32,)),
     ]
     return pl.pallas_call(
         functools.partial(kernel, nx, ny, nzc, top),
-        out_shape=jax.ShapeDtypeStruct((count, width // nx), BF16),
+        out_shape=pltpu.VMEM((count, width // nx), BF16),
         in_specs=[hbm] * (len(small_operands) + 5),
         out_specs=vmem,
         scratch_shapes=scratch,

time: 59.3 us -> 57 us (0.961)
  Pallas kernels: 57.8 us -> 56.2 us
  local copies, waits for them, and re-layouts: 1.3 us -> 0.6 us
    pallas_call x1, Pallas kernels: 57.8 us -> 56.2 us  [shards(): pl.pallas_call(functools.partial(kernel, nx, ny, nzc, top), out_shape=plt...]
    unnamed x1, local copies, waits for them, and re-layouts: 1.3 us -> 0.6 us
where the time goes in v4:
time: 57 us; the launch traced here: 56.8 us
  Pallas kernels  56.2 us (99%)
  local copies, waits for them, and re-layouts  0.6 us (1%)
    pallas_call x1, Pallas kernels, shards(): pl.pallas_call(functools.partial(kernel, nx, ny, nzc, top), out_shape=plt...  56.2 us

profile of v4, /device:TPU:1, one launch (start us, length us, event | category | flops | bytes accessed | tf_op | source)
XLA Modules:
  0.0 56.8 jit_solution(10384586495677997985)
XLA Ops:
  0.0 56.2 %decode_layer.1 = bf16[6,512]{1,0:T(8,128)(2,1)S(1)} custom-call(bf16[6,2048]{1,0:T(8,128)(2,1)} %residual_hbm.1, bf16[6,512]{1,0:T(8,128)(2,1)} %query_hbm.1, bf16[6,512]{1,0:T(8,128)(2,1)} %keys_hbm.1, bf16[6,1024]{1,0:T(8,128)(2,1)} %values_hbm.1, bf16[6,1024]{1,0:T(8,128)(2,1)} %out_gate_hbm.1, f32[6,8]{1,0:T(8,128)} %beta_logit_hbm.1, ...), custom_call_target="tpu_custom_call" | custom-call | tf_op jit(solution)/shard_map/decode_layer/pallas_call | solution.py:680
  56.2 0.6 %copy.22 = bf16[6,512]{1,0:T(8,128)(2,1)} copy(bf16[6,512]{1,0:T(8,128)(2,1)S(1)} %decode_layer.1) | data formatting | bytes 12288

commit v5 on v4

--- a/solution.py
+++ b/solution.py
@@ -148,8 +148,9 @@
 
     xs = [lax.rem(my_x + d, nx) for d in range(1, nx)]
     near_first = xs[0:1] + xs[2:] + xs[1:2]
-    ys = [lax.rem(my_y + d, ny) for d in range(1, ny)]
-    zs = [lax.rem(my_z + d, nz) for d in range(1, nz)]
+    far_first = xs[1:2] + xs[0:1] + xs[2:]
+    ys = [lax.rem(my_y + d, ny) for d in Y_ORDER if d]
+    zs = [lax.rem(my_z + d, nz) for d in Y_ORDER if d]
     zcs = [lax.rem(my_zc + d, nzc) for d in range(1, nzc)]
     sibling = place_of(my_x, my_y, my_z, other)
 
@@ -321,21 +322,22 @@
     row = iota((4 * heads * PAD, 4 * heads * count), 0)
     col = iota((4 * heads * PAD, 4 * heads * count), 1)
     filled = jnp.bitwise_and(row, 7) < count
-    unpack = (col == jnp.right_shift(row, 3) * count + jnp.bitwise_and(row, 7)) & filled
+    from_source = jnp.bitwise_and(jnp.right_shift(row, 3), 3)
+    from_head = jnp.right_shift(row, 5)
+    unpack = filled & (
+        col == (from_source * heads + from_head) * count + jnp.bitwise_and(row, 7)
+    )
     unpack = unpack.astype(BF16)
     whole_wait(g_in.at[pl.ds(0, 2 * ny - 1)], recv_sem.at[2])
     for n in range(0, 2 * ny, 4):
         four = mm(unpack, g_in[n : n + 4].reshape(4 * heads * count, LANES))
-        g_all[n : n + 4] = four.astype(BF16).reshape(4, heads * PAD, LANES)
-    first = jnp.zeros((2 * ny * 16, cols), F32)
-    second = jnp.zeros((2 * ny * 16, cols), F32)
+        g_all[:, n * PAD : (n + 4) * PAD] = four.astype(BF16).reshape(heads, 4 * PAD, LANES)
+    part = jnp.zeros((2 * ny * PAD, cols), F32)
     for g in range(key_heads):
-        rows = g_all[:, g * 16 : (g + 1) * 16, :].reshape(2 * ny * 16, LANES)
-        first += mm(rows, w_out[:, 2 * g * LANES : (2 * g + 1) * LANES], NT)
-        second += mm(rows, w_out[:, (2 * g + 1) * LANES : (2 * g + 2) * LANES], NT)
-    part = first.reshape(2 * ny, 2, PAD, cols)[:, 0] + second.reshape(2 * ny, 2, PAD, cols)[:, 1]
+        rows = jnp.concatenate([g_all[2 * g], g_all[2 * g + 1]], axis=1)
+        part += mm(rows, w_out[:, 2 * g * LANES : 2 * (g + 1) * LANES], NT)
     p_src[...] = part.reshape(2, nx, ROWS, cols)
-    for x in xs:
+    for x in far_first:
         for c in (my_c, other):
             send(p_src.at[c, x], p_in.at[my_c * nx + my_x], 4, place_of(x, my_y, my_z, c))
     send(p_src.at[other, my_x], p_in.at[my_c * nx + my_x], 4, sibling)
@@ -522,7 +524,7 @@
             up = both[:, (2 + e) * LANES : (3 + e) * LANES]
             hidden = hidden + silu(gate) * up * masks[e, n * block : (n + 1) * block]
         h_src[n] = hidden.astype(BF16)
-        for x in near_first:
+        for x in far_first:
             send(h_src.at[n], h_in.at[n, my_x], 28 + n, place_of(x, my_y, my_z, my_c))
         h_in[n, my_x] = h_src[n]
 
@@ -656,7 +658,7 @@
         pltpu.VMEM((heads * PAD, LANES), BF16),
         pltpu.VMEM((heads * count, LANES), BF16),
         pltpu.VMEM((2 * ny, heads * count, LANES), BF16),
-        pltpu.VMEM((2 * ny, heads * PAD, LANES), BF16),
+        pltpu.VMEM((heads, 2 * ny * PAD, LANES), BF16),
         pltpu.VMEM((2, nx, ROWS, cols), F32),
         pltpu.VMEM((2 * nx, ROWS, cols), F32),
         pltpu.VMEM((SRC, y_chunks * PAD, LANES), BF16),

time: 57 us -> 55.9 us (0.981)
  Pallas kernels: 56.2 us -> 55.2 us
    pallas_call x1, Pallas kernels: 56.2 us -> 55.2 us  [shards(): pl.pallas_call(functools.partial(kernel, nx, ny, nzc, top), out_shape=plt...]
where the time goes in v5:
time: 55.9 us; the launch traced here: 55.8 us
  Pallas kernels  55.2 us (99%)
  local copies, waits for them, and re-layouts  0.6 us (1%)
    pallas_call x1, Pallas kernels, shards(): pl.pallas_call(functools.partial(kernel, nx, ny, nzc, top), out_shape=plt...  55.2 us

profile of v5, /device:TPU:1, one launch (start us, length us, event | category | flops | bytes accessed | tf_op | source)
XLA Modules:
  0.0 55.8 jit_solution(18084097416328689544)
XLA Ops:
  0.0 55.2 %decode_layer.1 = bf16[6,512]{1,0:T(8,128)(2,1)S(1)} custom-call(bf16[6,2048]{1,0:T(8,128)(2,1)} %residual_hbm.1, bf16[6,512]{1,0:T(8,128)(2,1)} %query_hbm.1, bf16[6,512]{1,0:T(8,128)(2,1)} %keys_hbm.1, bf16[6,1024]{1,0:T(8,128)(2,1)} %values_hbm.1, bf16[6,1024]{1,0:T(8,128)(2,1)} %out_gate_hbm.1, f32[6,8]{1,0:T(8,128)} %beta_logit_hbm.1, ...), custom_call_target="tpu_custom_call" | custom-call | tf_op jit(solution)/shard_map/decode_layer/pallas_call | solution.py:682
  55.2 0.6 %copy.22 = bf16[6,512]{1,0:T(8,128)(2,1)} copy(bf16[6,512]{1,0:T(8,128)(2,1)S(1)} %decode_layer.1) | data formatting | bytes 12288

commit v6 on v5

--- a/solution.py
+++ b/solution.py
@@ -417,8 +417,8 @@
 
     m3_src[...] = mm(place[...], carried).astype(BF16).reshape(owners, 4, LANES)
     for i, z in enumerate(z_to):
-        for c in (my_c, other):
-            for dy in Y_ORDER:
+        for dy in Y_ORDER:
+            for c in (other, my_c):
                 y = lax.rem(my_y + dy, ny)
                 to = place_of(my_x, y, z, c)
                 src = m3_src.at[to[0]]
@@ -546,9 +546,9 @@
         ]
         turned = mm(flatten, jnp.concatenate(tiles, axis=0).astype(BF16)).astype(BF16)
         m6_src[n * g_zc : (n + 1) * g_zc] = turned.reshape(g_zc, ny, 4, LANES)
-        for i in range(n * GROUP_Z, (n + 1) * GROUP_Z):
-            for c in (my_c, other):
-                for dy in Y_ORDER:
+        for i in reversed(range(n * GROUP_Z, (n + 1) * GROUP_Z)):
+            for dy in Y_ORDER:
+                for c in (other, my_c):
                     y = lax.rem(my_y + dy, ny)
                     src = m6_src.at[i * 2 + c, y]
                     if order[i] or dy or c is other:

time: 55.9 us -> 55.3 us (0.989)
  Pallas kernels: 55.2 us -> 54.6 us
    pallas_call x1, Pallas kernels: 55.2 us -> 54.6 us  [shards(): pl.pallas_call(functools.partial(kernel, nx, ny, nzc, top), out_shape=plt...]
where the time goes in v6:
time: 55.3 us; the launch traced here: 55.2 us
  Pallas kernels  54.6 us (99%)
  local copies, waits for them, and re-layouts  0.6 us (1%)
    pallas_call x1, Pallas kernels, shards(): pl.pallas_call(functools.partial(kernel, nx, ny, nzc, top), out_shape=plt...  54.6 us

profile of v6, /device:TPU:1, one launch (start us, length us, event | category | flops | bytes accessed | tf_op | source)
XLA Modules:
  0.0 55.2 jit_solution(11801260393845661718)
XLA Ops:
  0.0 54.6 %decode_layer.1 = bf16[6,512]{1,0:T(8,128)(2,1)S(1)} custom-call(bf16[6,2048]{1,0:T(8,128)(2,1)} %residual_hbm.1, bf16[6,512]{1,0:T(8,128)(2,1)} %query_hbm.1, bf16[6,512]{1,0:T(8,128)(2,1)} %keys_hbm.1, bf16[6,1024]{1,0:T(8,128)(2,1)} %values_hbm.1, bf16[6,1024]{1,0:T(8,128)(2,1)} %out_gate_hbm.1, f32[6,8]{1,0:T(8,128)} %beta_logit_hbm.1, ...), custom_call_target="tpu_custom_call" | custom-call | tf_op jit(solution)/shard_map/decode_layer/pallas_call | solution.py:682
  54.6 0.6 %copy.22 = bf16[6,512]{1,0:T(8,128)(2,1)} copy(bf16[6,512]{1,0:T(8,128)(2,1)S(1)} %decode_layer.1) | data formatting | bytes 12288
